TPU v7x, 512 devices: a whole 4x8x8 slice. The times are simulated.
512 devices in a mesh: store: 32 (over z, y_lo, core), prod: 16 (over y_hi, x).
Axes of the slice: x: 4, y: 8 (y_hi: 4, y_lo: 2; y = y_hi * 2 + y_lo), z: 8, core: 2. Of those that a mesh axis runs over, the one named last changes fastest.
Arguments:
- gradients: bfloat16 [196608, 2048], P(('store', 'prod')), may hold values from -6 to 6
- destinations: int32 [196608], P(('store', 'prod')), may hold values from 0 to 31, as said below
- queries: bfloat16 [1536, 2048], P(('store', 'prod')), may hold values from -6 to 6
- left_factor: float32 [32, 32], replicated, may hold values from -11 to 11, as said below
- right_factor: float32 [64, 64], replicated, may hold values from -11 to 11, as said below
Outputs:
- scores: bfloat16 [1536, 393216], P(None, ('store', 'prod'))
Inputs may be any that keep to these rules, and one draw needn't show every extreme that they name: `destinations`: within the rows of one producer (aligned blocks of 384 rows) no store index is named more than 24 times, and one store index, the same for every producer, is named exactly 24 times in every block. `left_factor`: a dense real matrix. `right_factor`: a dense real matrix.
All inputs are finite; a program needn't handle non-finite values.
Results may differ from a plain program's by a relative error of at most 0.0049.
Values may be sent and summed in bfloat16 or wider, within the bound.
No kernel may reach another device: no remote copies, remote signals or barrier semaphores. Data moves between devices by JAX's collectives and lax.ppermute only.
A program may use at most 64 MiB of HBM per device.

v0:
```python
import math

import jax
import jax.numpy as jnp
from jax import lax
from jax.sharding import PartitionSpec as P


def from_behind(block, axis, distance):
    devices = range(lax.axis_size(axis))
    route = [((i - distance) % len(devices), i) for i in devices]
    return lax.ppermute(block, axis, route)


def precondition(gradients, left_factor, right_factor):
    left_size = left_factor.shape[0]
    right_size = right_factor.shape[0]
    leading = gradients.shape[:-1]
    matrices = gradients.astype(jnp.float32).reshape((-1, left_size, right_size))
    right_done = jnp.einsum("nbc,cd->nbd", matrices, right_factor, precision=lax.Precision.HIGHEST)
    product = jnp.einsum("ab,nbd->nad", left_factor, right_done, precision=lax.Precision.HIGHEST)
    product = product.reshape(leading + (left_size * right_size,))
    scaling = lax.rsqrt(jnp.mean(product * product, axis=-1, keepdims=True) + 1e-06)
    return (product * scaling * (1.0 / math.sqrt(left_size * right_size))).astype(jnp.bfloat16)


def row_ranks(targets, owners):
    matches = (targets[:, None] == jnp.arange(owners, dtype=jnp.int32)[None, :]).astype(jnp.int32)
    earlier = jnp.cumsum(matches, axis=0) - matches
    return jnp.sum(earlier * matches, axis=1)


def fill_tile(scores, local_block, position, stored):
    product = lax.dot_general(
        local_block, stored, (((1,), (1,)), ((), ())), preferred_element_type=jnp.float32
    )
    return lax.dynamic_update_slice_in_dim(
        scores, product.astype(jnp.bfloat16), position * local_block.shape[0], 0
    )


def body(gradients, destinations, queries, left_factor, right_factor):
    owners = lax.axis_size("store")
    own_index = lax.axis_index("store")
    row_count, feature_width = gradients.shape
    bucket = 2 * row_count // owners
    capacity = owners * bucket
    places = destinations * bucket + row_ranks(destinations, owners)
    local_queries = lax.all_gather(queries, "prod", axis=0, tiled=True)
    blank_scores = jnp.zeros((local_queries.shape[0] * owners, capacity), jnp.bfloat16)
    buffer = jnp.zeros((capacity, feature_width), jnp.bfloat16).at[places].set(gradients)
    buffer = buffer.reshape((owners, bucket, feature_width))
    stored = precondition(
        lax.all_to_all(buffer, "store", split_axis=0, concat_axis=0, tiled=True),
        left_factor,
        right_factor,
    ).reshape((capacity, feature_width))
    scores = fill_tile(blank_scores, local_queries, own_index, stored)

    def advance(turn_index, cycle_state):
        current, moving = cycle_state
        moving = from_behind(moving, "store", 1)
        current = fill_tile(current, moving, (own_index - turn_index) % owners, stored)
        return (current, moving)

    scores, moving = lax.fori_loop(1, owners, advance, (scores, local_queries))
    return scores


def solution(mesh):
    return jax.shard_map(
        body,
        mesh=mesh,
        in_specs=(
            P(("store", "prod"), None),
            P(("store", "prod")),
            P(("store", "prod"), None),
            P(),
            P(),
        ),
        out_specs=P(None, ("store", "prod")),
        check_vma=False,
    )
```

profile of v0, /device:TPU:6, one launch (start us, length us, event | category | flops | bytes accessed | tf_op | source)
XLA Modules:
  0.0 511.0 jit_solution(16796309453098849389)
XLA Ops:
  9.2 11.9 %all-to-all-start = ((bf16[32,24,2048]{2,1,0:T(8,128)(2,1)}), bf16[32,24,2048]{2,1,0:T(8,128)(2,1)S(1)}, u32[]{:S(2)}, u32[]{:S(2)}) async-start(bf16[32,24,2048]{2,1,0:T(8,128)(2,1)} %bitcast.2), calls=%async_computation | async-start | bytes 6291456 | tf_op jit(solution)/shard_map/all_to_all | solution.py:54
  21.0 86.9 %all-gather = bf16[16,3,2048]{2,1,0:T(4,128)(2,1)S(1)} all-gather(bf16[1,3,2048]{2,1,0:T(4,128)(2,1)S(1)} %bitcast.52), channel_id=1, replica_groups=mesh['store'=32,'prod'=16] {'prod'}, dimensions={0}, use_global_device_ids=true | all-gather | bytes 208896 | tf_op jit(solution)/shard_map/all_gather | solution.py:49
  108.8 7.6 %reshape.42 = bf16[768,32,64]{2,1,0:T(8,128)(2,1)} reshape(bf16[32,24,2048]{2,1,0:T(8,128)(2,1)S(1)} %all-to-all-done) | data formatting | bytes 6291456 | tf_op jit(solution)/shard_map/reshape | solution.py:19
  116.4 9.0 %fusion.5 = f32[768,32,64]{0,2,1:T(8,128)S(1)} fusion(bf16[768,32,64]{2,1,0:T(8,128)(2,1)} %reshape.42, f32[64,64]{1,0:T(8,128)S(1)} %copy-done), kind=kOutput, calls=%fused_computation.8 | convolution fusion | flops 1207959552 | bytes 9453568 | tf_op jit(solution)/shard_map/nbc,cd->nbd/dot_general | solution.py:20
  125.5 10.1 %multiply_reduce_fusion = (f32[768]{0:T(1024)S(1)}, f32[768,32,64]{0,1,2:T(8,128)S(1)}) fusion(f32[32,32]{1,0:T(8,128)S(1)} %copy-done.2, f32[768,32,64]{0,2,1:T(8,128)S(1)} %fusion.5), kind=kOutput, calls=%fused_computation.10 | convolution fusion | flops 607124736 | bytes 12590080 | tf_op jit(solution)/shard_map/ab,nbd->nad/dot_general | solution.py:21
  149.3 361.7 %while.17 = (s32[]{:T(128)}, bf16[1536,768]{1,0:T(8,128)(2,1)}, bf16[48,2048]{1,0:T(8,128)(2,1)}, bf16[768,2048]{1,0:T(8,128)(2,1)S(1)}, s32[]{:T(128)}, /*index...) while((s32[]{:T(128)}, bf16[1536,768]{1,0:T(8,128)(2,1)}, ...), condition=%wide.region_6.7_spmd, body=%wide.region_5.6_spmd.sunk | while | flops 151031824 | bytes 4596032 | solution.py:66
  151.2 7.4 %collective-permute-done = bf16[48,2048]{1,0:T(8,128)(2,1)S(1)} collective-permute-done((bf16[48,2048]{1,0:T(8,128)(2,1)}, bf16[48,2048]{1,0:T(8,128)(2,1)S(1)}, u32[]{:S(2)}, u32[]{:S(2)}) %collective-permute-start) | collective-permute-done | bytes 196640 | tf_op jit(solution)/shard_map/while/body/eval_jaxpr/ppermute | solution.py:12
  174.6 7.4 %collective-permute-done = bf16[48,2048]{1,0:T(8,128)(2,1)S(1)} collective-permute-done((bf16[48,2048]{1,0:T(8,128)(2,1)}, bf16[48,2048]{1,0:T(8,128)(2,1)S(1)}, u32[]{:S(2)}, u32[]{:S(2)}) %collective-permute-start) | collective-permute-done | bytes 196640 | tf_op jit(solution)/shard_map/while/body/eval_jaxpr/ppermute | solution.py:12
  197.9 7.4 %collective-permute-done = bf16[48,2048]{1,0:T(8,128)(2,1)S(1)} collective-permute-done((bf16[48,2048]{1,0:T(8,128)(2,1)}, bf16[48,2048]{1,0:T(8,128)(2,1)S(1)}, u32[]{:S(2)}, u32[]{:S(2)}) %collective-permute-start) | collective-permute-done | bytes 196640 | tf_op jit(solution)/shard_map/while/body/eval_jaxpr/ppermute | solution.py:12
  209.6 7.4 %collective-permute-done = bf16[48,2048]{1,0:T(8,128)(2,1)S(1)} collective-permute-done((bf16[48,2048]{1,0:T(8,128)(2,1)}, bf16[48,2048]{1,0:T(8,128)(2,1)S(1)}, u32[]{:S(2)}, u32[]{:S(2)}) %collective-permute-start) | collective-permute-done | bytes 196640 | tf_op jit(solution)/shard_map/while/body/eval_jaxpr/ppermute | solution.py:12
  221.2 7.4 %collective-permute-done = bf16[48,2048]{1,0:T(8,128)(2,1)S(1)} collective-permute-done((bf16[48,2048]{1,0:T(8,128)(2,1)}, bf16[48,2048]{1,0:T(8,128)(2,1)S(1)}, u32[]{:S(2)}, u32[]{:S(2)}) %collective-permute-start) | collective-permute-done | bytes 196640 | tf_op jit(solution)/shard_map/while/body/eval_jaxpr/ppermute | solution.py:12
  232.9 7.4 %collective-permute-done = bf16[48,2048]{1,0:T(8,128)(2,1)S(1)} collective-permute-done((bf16[48,2048]{1,0:T(8,128)(2,1)}, bf16[48,2048]{1,0:T(8,128)(2,1)S(1)}, u32[]{:S(2)}, u32[]{:S(2)}) %collective-permute-start) | collective-permute-done | bytes 196640 | tf_op jit(solution)/shard_map/while/body/eval_jaxpr/ppermute | solution.py:12
  244.6 7.4 %collective-permute-done = bf16[48,2048]{1,0:T(8,128)(2,1)S(1)} collective-permute-done((bf16[48,2048]{1,0:T(8,128)(2,1)}, bf16[48,2048]{1,0:T(8,128)(2,1)S(1)}, u32[]{:S(2)}, u32[]{:S(2)}) %collective-permute-start) | collective-permute-done | bytes 196640 | tf_op jit(solution)/shard_map/while/body/eval_jaxpr/ppermute | solution.py:12
  267.9 7.4 %collective-permute-done = bf16[48,2048]{1,0:T(8,128)(2,1)S(1)} collective-permute-done((bf16[48,2048]{1,0:T(8,128)(2,1)}, bf16[48,2048]{1,0:T(8,128)(2,1)S(1)}, u32[]{:S(2)}, u32[]{:S(2)}) %collective-permute-start) | collective-permute-done | bytes 196640 | tf_op jit(solution)/shard_map/while/body/eval_jaxpr/ppermute | solution.py:12
  279.6 7.4 %collective-permute-done = bf16[48,2048]{1,0:T(8,128)(2,1)S(1)} collective-permute-done((bf16[48,2048]{1,0:T(8,128)(2,1)}, bf16[48,2048]{1,0:T(8,128)(2,1)S(1)}, u32[]{:S(2)}, u32[]{:S(2)}) %collective-permute-start) | collective-permute-done | bytes 196640 | tf_op jit(solution)/shard_map/while/body/eval_jaxpr/ppermute | solution.py:12
  291.2 7.4 %collective-permute-done = bf16[48,2048]{1,0:T(8,128)(2,1)S(1)} collective-permute-done((bf16[48,2048]{1,0:T(8,128)(2,1)}, bf16[48,2048]{1,0:T(8,128)(2,1)S(1)}, u32[]{:S(2)}, u32[]{:S(2)}) %collective-permute-start) | collective-permute-done | bytes 196640 | tf_op jit(solution)/shard_map/while/body/eval_jaxpr/ppermute | solution.py:12
  302.9 7.4 %collective-permute-done = bf16[48,2048]{1,0:T(8,128)(2,1)S(1)} collective-permute-done((bf16[48,2048]{1,0:T(8,128)(2,1)}, bf16[48,2048]{1,0:T(8,128)(2,1)S(1)}, u32[]{:S(2)}, u32[]{:S(2)}) %collective-permute-start) | collective-permute-done | bytes 196640 | tf_op jit(solution)/shard_map/while/body/eval_jaxpr/ppermute | solution.py:12
  314.6 7.4 %collective-permute-done = bf16[48,2048]{1,0:T(8,128)(2,1)S(1)} collective-permute-done((bf16[48,2048]{1,0:T(8,128)(2,1)}, bf16[48,2048]{1,0:T(8,128)(2,1)S(1)}, u32[]{:S(2)}, u32[]{:S(2)}) %collective-permute-start) | collective-permute-done | bytes 196640 | tf_op jit(solution)/shard_map/while/body/eval_jaxpr/ppermute | solution.py:12
  326.2 7.4 %collective-permute-done = bf16[48,2048]{1,0:T(8,128)(2,1)S(1)} collective-permute-done((bf16[48,2048]{1,0:T(8,128)(2,1)}, bf16[48,2048]{1,0:T(8,128)(2,1)S(1)}, u32[]{:S(2)}, u32[]{:S(2)}) %collective-permute-start) | collective-permute-done | bytes 196640 | tf_op jit(solution)/shard_map/while/body/eval_jaxpr/ppermute | solution.py:12
  337.9 7.4 %collective-permute-done = bf16[48,2048]{1,0:T(8,128)(2,1)S(1)} collective-permute-done((bf16[48,2048]{1,0:T(8,128)(2,1)}, bf16[48,2048]{1,0:T(8,128)(2,1)S(1)}, u32[]{:S(2)}, u32[]{:S(2)}) %collective-permute-start) | collective-permute-done | bytes 196640 | tf_op jit(solution)/shard_map/while/body/eval_jaxpr/ppermute | solution.py:12
  349.6 7.4 %collective-permute-done = bf16[48,2048]{1,0:T(8,128)(2,1)S(1)} collective-permute-done((bf16[48,2048]{1,0:T(8,128)(2,1)}, bf16[48,2048]{1,0:T(8,128)(2,1)S(1)}, u32[]{:S(2)}, u32[]{:S(2)}) %collective-permute-start) | collective-permute-done | bytes 196640 | tf_op jit(solution)/shard_map/while/body/eval_jaxpr/ppermute | solution.py:12
  361.2 7.4 %collective-permute-done = bf16[48,2048]{1,0:T(8,128)(2,1)S(1)} collective-permute-done((bf16[48,2048]{1,0:T(8,128)(2,1)}, bf16[48,2048]{1,0:T(8,128)(2,1)S(1)}, u32[]{:S(2)}, u32[]{:S(2)}) %collective-permute-start) | collective-permute-done | bytes 196640 | tf_op jit(solution)/shard_map/while/body/eval_jaxpr/ppermute | solution.py:12
  372.9 7.4 %collective-permute-done = bf16[48,2048]{1,0:T(8,128)(2,1)S(1)} collective-permute-done((bf16[48,2048]{1,0:T(8,128)(2,1)}, bf16[48,2048]{1,0:T(8,128)(2,1)S(1)}, u32[]{:S(2)}, u32[]{:S(2)}) %collective-permute-start) | collective-permute-done | bytes 196640 | tf_op jit(solution)/shard_map/while/body/eval_jaxpr/ppermute | solution.py:12
  407.9 7.4 %collective-permute-done = bf16[48,2048]{1,0:T(8,128)(2,1)S(1)} collective-permute-done((bf16[48,2048]{1,0:T(8,128)(2,1)}, bf16[48,2048]{1,0:T(8,128)(2,1)S(1)}, u32[]{:S(2)}, u32[]{:S(2)}) %collective-permute-start) | collective-permute-done | bytes 196640 | tf_op jit(solution)/shard_map/while/body/eval_jaxpr/ppermute | solution.py:12
  (129 shorter events, 251.8 us)
Async XLA Ops:
  9.2 99.6 %all-to-all-start = ((bf16[32,24,2048]{2,1,0:T(8,128)(2,1)}), bf16[32,24,2048]{2,1,0:T(8,128)(2,1)S(1)}, u32[]{:S(2)}, u32[]{:S(2)}) async-start(bf16[32,24,2048]{2,1,0:T(8,128)(2,1)} %bitcast.2), calls=%async_computation | async-start | bytes 6291456 | tf_op jit(solution)/shard_map/all_to_all | solution.py:54
  149.3 9.3 %collective-permute-start = (bf16[48,2048]{1,0:T(8,128)(2,1)}, bf16[48,2048]{1,0:T(8,128)(2,1)S(1)}, u32[]{:S(2)}, u32[]{:S(2)}) collective-permute-start(bf16[48,2048]{1,0:T(8,128)(2,1)} %get-tuple-element.205), channel_id=1, source_target_pairs={{496,0},{0,16},{16,32},{32,48},{48,64},{64,80},{80,96},{96,112},{1... | collective-permute-start | bytes 589832 | tf_op jit(solution)/shard_map/while/body/eval_jaxpr/ppermute | solution.py:12
  172.6 9.3 %collective-permute-start = (bf16[48,2048]{1,0:T(8,128)(2,1)}, bf16[48,2048]{1,0:T(8,128)(2,1)S(1)}, u32[]{:S(2)}, u32[]{:S(2)}) collective-permute-start(bf16[48,2048]{1,0:T(8,128)(2,1)} %get-tuple-element.205), channel_id=1, source_target_pairs={{496,0},{0,16},{16,32},{32,48},{48,64},{64,80},{80,96},{96,112},{1... | collective-permute-start | bytes 589832 | tf_op jit(solution)/shard_map/while/body/eval_jaxpr/ppermute | solution.py:12
  196.0 9.3 %collective-permute-start = (bf16[48,2048]{1,0:T(8,128)(2,1)}, bf16[48,2048]{1,0:T(8,128)(2,1)S(1)}, u32[]{:S(2)}, u32[]{:S(2)}) collective-permute-start(bf16[48,2048]{1,0:T(8,128)(2,1)} %get-tuple-element.205), channel_id=1, source_target_pairs={{496,0},{0,16},{16,32},{32,48},{48,64},{64,80},{80,96},{96,112},{1... | collective-permute-start | bytes 589832 | tf_op jit(solution)/shard_map/while/body/eval_jaxpr/ppermute | solution.py:12
  207.6 9.3 %collective-permute-start = (bf16[48,2048]{1,0:T(8,128)(2,1)}, bf16[48,2048]{1,0:T(8,128)(2,1)S(1)}, u32[]{:S(2)}, u32[]{:S(2)}) collective-permute-start(bf16[48,2048]{1,0:T(8,128)(2,1)} %get-tuple-element.205), channel_id=1, source_target_pairs={{496,0},{0,16},{16,32},{32,48},{48,64},{64,80},{80,96},{96,112},{1... | collective-permute-start | bytes 589832 | tf_op jit(solution)/shard_map/while/body/eval_jaxpr/ppermute | solution.py:12
  219.3 9.3 %collective-permute-start = (bf16[48,2048]{1,0:T(8,128)(2,1)}, bf16[48,2048]{1,0:T(8,128)(2,1)S(1)}, u32[]{:S(2)}, u32[]{:S(2)}) collective-permute-start(bf16[48,2048]{1,0:T(8,128)(2,1)} %get-tuple-element.205), channel_id=1, source_target_pairs={{496,0},{0,16},{16,32},{32,48},{48,64},{64,80},{80,96},{96,112},{1... | collective-permute-start | bytes 589832 | tf_op jit(solution)/shard_map/while/body/eval_jaxpr/ppermute | solution.py:12
  231.0 9.3 %collective-permute-start = (bf16[48,2048]{1,0:T(8,128)(2,1)}, bf16[48,2048]{1,0:T(8,128)(2,1)S(1)}, u32[]{:S(2)}, u32[]{:S(2)}) collective-permute-start(bf16[48,2048]{1,0:T(8,128)(2,1)} %get-tuple-element.205), channel_id=1, source_target_pairs={{496,0},{0,16},{16,32},{32,48},{48,64},{64,80},{80,96},{96,112},{1... | collective-permute-start | bytes 589832 | tf_op jit(solution)/shard_map/while/body/eval_jaxpr/ppermute | solution.py:12
  242.6 9.3 %collective-permute-start = (bf16[48,2048]{1,0:T(8,128)(2,1)}, bf16[48,2048]{1,0:T(8,128)(2,1)S(1)}, u32[]{:S(2)}, u32[]{:S(2)}) collective-permute-start(bf16[48,2048]{1,0:T(8,128)(2,1)} %get-tuple-element.205), channel_id=1, source_target_pairs={{496,0},{0,16},{16,32},{32,48},{48,64},{64,80},{80,96},{96,112},{1... | collective-permute-start | bytes 589832 | tf_op jit(solution)/shard_map/while/body/eval_jaxpr/ppermute | solution.py:12
  266.0 9.3 %collective-permute-start = (bf16[48,2048]{1,0:T(8,128)(2,1)}, bf16[48,2048]{1,0:T(8,128)(2,1)S(1)}, u32[]{:S(2)}, u32[]{:S(2)}) collective-permute-start(bf16[48,2048]{1,0:T(8,128)(2,1)} %get-tuple-element.205), channel_id=1, source_target_pairs={{496,0},{0,16},{16,32},{32,48},{48,64},{64,80},{80,96},{96,112},{1... | collective-permute-start | bytes 589832 | tf_op jit(solution)/shard_map/while/body/eval_jaxpr/ppermute | solution.py:12
  289.3 9.3 %collective-permute-start = (bf16[48,2048]{1,0:T(8,128)(2,1)}, bf16[48,2048]{1,0:T(8,128)(2,1)S(1)}, u32[]{:S(2)}, u32[]{:S(2)}) collective-permute-start(bf16[48,2048]{1,0:T(8,128)(2,1)} %get-tuple-element.205), channel_id=1, source_target_pairs={{496,0},{0,16},{16,32},{32,48},{48,64},{64,80},{80,96},{96,112},{1... | collective-permute-start | bytes 589832 | tf_op jit(solution)/shard_map/while/body/eval_jaxpr/ppermute | solution.py:12
  301.0 9.3 %collective-permute-start = (bf16[48,2048]{1,0:T(8,128)(2,1)}, bf16[48,2048]{1,0:T(8,128)(2,1)S(1)}, u32[]{:S(2)}, u32[]{:S(2)}) collective-permute-start(bf16[48,2048]{1,0:T(8,128)(2,1)} %get-tuple-element.205), channel_id=1, source_target_pairs={{496,0},{0,16},{16,32},{32,48},{48,64},{64,80},{80,96},{96,112},{1... | collective-permute-start | bytes 589832 | tf_op jit(solution)/shard_map/while/body/eval_jaxpr/ppermute | solution.py:12
  312.6 9.3 %collective-permute-start = (bf16[48,2048]{1,0:T(8,128)(2,1)}, bf16[48,2048]{1,0:T(8,128)(2,1)S(1)}, u32[]{:S(2)}, u32[]{:S(2)}) collective-permute-start(bf16[48,2048]{1,0:T(8,128)(2,1)} %get-tuple-element.205), channel_id=1, source_target_pairs={{496,0},{0,16},{16,32},{32,48},{48,64},{64,80},{80,96},{96,112},{1... | collective-permute-start | bytes 589832 | tf_op jit(solution)/shard_map/while/body/eval_jaxpr/ppermute | solution.py:12
  324.3 9.3 %collective-permute-start = (bf16[48,2048]{1,0:T(8,128)(2,1)}, bf16[48,2048]{1,0:T(8,128)(2,1)S(1)}, u32[]{:S(2)}, u32[]{:S(2)}) collective-permute-start(bf16[48,2048]{1,0:T(8,128)(2,1)} %get-tuple-element.205), channel_id=1, source_target_pairs={{496,0},{0,16},{16,32},{32,48},{48,64},{64,80},{80,96},{96,112},{1... | collective-permute-start | bytes 589832 | tf_op jit(solution)/shard_map/while/body/eval_jaxpr/ppermute | solution.py:12
  336.0 9.3 %collective-permute-start = (bf16[48,2048]{1,0:T(8,128)(2,1)}, bf16[48,2048]{1,0:T(8,128)(2,1)S(1)}, u32[]{:S(2)}, u32[]{:S(2)}) collective-permute-start(bf16[48,2048]{1,0:T(8,128)(2,1)} %get-tuple-element.205), channel_id=1, source_target_pairs={{496,0},{0,16},{16,32},{32,48},{48,64},{64,80},{80,96},{96,112},{1... | collective-permute-start | bytes 589832 | tf_op jit(solution)/shard_map/while/body/eval_jaxpr/ppermute | solution.py:12
  347.6 9.3 %collective-permute-start = (bf16[48,2048]{1,0:T(8,128)(2,1)}, bf16[48,2048]{1,0:T(8,128)(2,1)S(1)}, u32[]{:S(2)}, u32[]{:S(2)}) collective-permute-start(bf16[48,2048]{1,0:T(8,128)(2,1)} %get-tuple-element.205), channel_id=1, source_target_pairs={{496,0},{0,16},{16,32},{32,48},{48,64},{64,80},{80,96},{96,112},{1... | collective-permute-start | bytes 589832 | tf_op jit(solution)/shard_map/while/body/eval_jaxpr/ppermute | solution.py:12
  359.3 9.3 %collective-permute-start = (bf16[48,2048]{1,0:T(8,128)(2,1)}, bf16[48,2048]{1,0:T(8,128)(2,1)S(1)}, u32[]{:S(2)}, u32[]{:S(2)}) collective-permute-start(bf16[48,2048]{1,0:T(8,128)(2,1)} %get-tuple-element.205), channel_id=1, source_target_pairs={{496,0},{0,16},{16,32},{32,48},{48,64},{64,80},{80,96},{96,112},{1... | collective-permute-start | bytes 589832 | tf_op jit(solution)/shard_map/while/body/eval_jaxpr/ppermute | solution.py:12
  371.0 9.3 %collective-permute-start = (bf16[48,2048]{1,0:T(8,128)(2,1)}, bf16[48,2048]{1,0:T(8,128)(2,1)S(1)}, u32[]{:S(2)}, u32[]{:S(2)}) collective-permute-start(bf16[48,2048]{1,0:T(8,128)(2,1)} %get-tuple-element.205), channel_id=1, source_target_pairs={{496,0},{0,16},{16,32},{32,48},{48,64},{64,80},{80,96},{96,112},{1... | collective-permute-start | bytes 589832 | tf_op jit(solution)/shard_map/while/body/eval_jaxpr/ppermute | solution.py:12
  406.0 9.3 %collective-permute-start = (bf16[48,2048]{1,0:T(8,128)(2,1)}, bf16[48,2048]{1,0:T(8,128)(2,1)S(1)}, u32[]{:S(2)}, u32[]{:S(2)}) collective-permute-start(bf16[48,2048]{1,0:T(8,128)(2,1)} %get-tuple-element.205), channel_id=1, source_target_pairs={{496,0},{0,16},{16,32},{32,48},{48,64},{64,80},{80,96},{96,112},{1... | collective-permute-start | bytes 589832 | tf_op jit(solution)/shard_map/while/body/eval_jaxpr/ppermute | solution.py:12
  429.3 9.3 %collective-permute-start = (bf16[48,2048]{1,0:T(8,128)(2,1)}, bf16[48,2048]{1,0:T(8,128)(2,1)S(1)}, u32[]{:S(2)}, u32[]{:S(2)}) collective-permute-start(bf16[48,2048]{1,0:T(8,128)(2,1)} %get-tuple-element.205), channel_id=1, source_target_pairs={{496,0},{0,16},{16,32},{32,48},{48,64},{64,80},{80,96},{96,112},{1... | collective-permute-start | bytes 589832 | tf_op jit(solution)/shard_map/while/body/eval_jaxpr/ppermute | solution.py:12
  441.0 9.3 %collective-permute-start = (bf16[48,2048]{1,0:T(8,128)(2,1)}, bf16[48,2048]{1,0:T(8,128)(2,1)S(1)}, u32[]{:S(2)}, u32[]{:S(2)}) collective-permute-start(bf16[48,2048]{1,0:T(8,128)(2,1)} %get-tuple-element.205), channel_id=1, source_target_pairs={{496,0},{0,16},{16,32},{32,48},{48,64},{64,80},{80,96},{96,112},{1... | collective-permute-start | bytes 589832 | tf_op jit(solution)/shard_map/while/body/eval_jaxpr/ppermute | solution.py:12
  452.6 9.3 %collective-permute-start = (bf16[48,2048]{1,0:T(8,128)(2,1)}, bf16[48,2048]{1,0:T(8,128)(2,1)S(1)}, u32[]{:S(2)}, u32[]{:S(2)}) collective-permute-start(bf16[48,2048]{1,0:T(8,128)(2,1)} %get-tuple-element.205), channel_id=1, source_target_pairs={{496,0},{0,16},{16,32},{32,48},{48,64},{64,80},{80,96},{96,112},{1... | collective-permute-start | bytes 589832 | tf_op jit(solution)/shard_map/while/body/eval_jaxpr/ppermute | solution.py:12
  464.3 9.3 %collective-permute-start = (bf16[48,2048]{1,0:T(8,128)(2,1)}, bf16[48,2048]{1,0:T(8,128)(2,1)S(1)}, u32[]{:S(2)}, u32[]{:S(2)}) collective-permute-start(bf16[48,2048]{1,0:T(8,128)(2,1)} %get-tuple-element.205), channel_id=1, source_target_pairs={{496,0},{0,16},{16,32},{32,48},{48,64},{64,80},{80,96},{96,112},{1... | collective-permute-start | bytes 589832 | tf_op jit(solution)/shard_map/while/body/eval_jaxpr/ppermute | solution.py:12
  476.0 9.3 %collective-permute-start = (bf16[48,2048]{1,0:T(8,128)(2,1)}, bf16[48,2048]{1,0:T(8,128)(2,1)S(1)}, u32[]{:S(2)}, u32[]{:S(2)}) collective-permute-start(bf16[48,2048]{1,0:T(8,128)(2,1)} %get-tuple-element.205), channel_id=1, source_target_pairs={{496,0},{0,16},{16,32},{32,48},{48,64},{64,80},{80,96},{96,112},{1... | collective-permute-start | bytes 589832 | tf_op jit(solution)/shard_map/while/body/eval_jaxpr/ppermute | solution.py:12
  487.6 9.3 %collective-permute-start = (bf16[48,2048]{1,0:T(8,128)(2,1)}, bf16[48,2048]{1,0:T(8,128)(2,1)S(1)}, u32[]{:S(2)}, u32[]{:S(2)}) collective-permute-start(bf16[48,2048]{1,0:T(8,128)(2,1)} %get-tuple-element.205), channel_id=1, source_target_pairs={{496,0},{0,16},{16,32},{32,48},{48,64},{64,80},{80,96},{96,112},{1... | collective-permute-start | bytes 589832 | tf_op jit(solution)/shard_map/while/body/eval_jaxpr/ppermute | solution.py:12
  (12 other events, 213.1 us)
where the time goes:
time: 518 us; the launch traced here: 511 us
  waiting for transfers between devices  228 us (44%)
  blocking collectives  86.9 us (17%)
  matrix products  74.3 us (14%)
  starting transfers between devices  71 us (14%)
  local copies, waits for them, and re-layouts  44.1 us (9%)
  other arithmetic  5.48 us (1%)
    ppermute x31, waiting for transfers between devices, from_behind(): return lax.ppermute(block, axis, route)  228 us
    all_gather x1, blocking collectives, body(): local_queries = lax.all_gather(queries, 'prod', axis=0, tiled=True)  86.9 us
    ppermute x31, starting transfers between devices, from_behind(): return lax.ppermute(block, axis, route)  59.1 us
    dot_general x32, matrix products, fill_tile(): lax.dot_general(local_block, stored, (((1,), (1,)), ((), ())), preferred_...  55.2 us
    while x31, local copies, waits for them, and re-layouts  20.9 us
    all_to_all x1, starting transfers between devices, body(): lax.all_to_all(buffer, 'store', split_axis=0, concat_axis=0, tiled=True)  11.9 us
  transfers between devices with their start and end apart: 32, of which 31 were waited for; matrix products, arithmetic and copies ran while one was open for 0% of the time, Pallas kernels for 0%

commit v1 on v0

v1 whole, which is shorter than its diff:
```python
import math

import jax
import jax.numpy as jnp
from jax import lax
from jax.experimental import pallas as pl
from jax.experimental.pallas import tpu as pltpu
from jax.sharding import Mesh, PartitionSpec as P

STORE = ("z", "y_lo", "core")
PROD = ("y_hi", "x")
HIGHEST = lax.Precision.HIGHEST


def exchange(block, axis):
    return lax.all_to_all(block, axis, split_axis=0, concat_axis=0, tiled=True)


def gather(block, axis):
    count = lax.axis_size(axis)
    return exchange(jnp.broadcast_to(block[None], (count,) + block.shape), axis)


def kron(left, matrices, right):
    rows = matrices.shape[0]
    cubes = matrices.astype(jnp.float32).reshape((rows, left.shape[1], right.shape[0]))
    half = jnp.einsum("nbc,cd->nbd", cubes, right, precision=HIGHEST)
    return jnp.einsum("ab,nbd->nad", left, half, precision=HIGHEST)


def slots_of(targets, bucket):
    rows = targets.shape[1]
    above = lax.broadcasted_iota(jnp.int32, (rows, rows), 0)
    along = lax.broadcasted_iota(jnp.int32, (rows, rows), 1)
    upright = jnp.sum(jnp.where(above == along, targets, 0), axis=1, keepdims=True)
    earlier = jnp.where((upright == targets) & (above < along), 1, 0)
    return targets * bucket + jnp.sum(earlier, axis=0, keepdims=True)


def place(gradients, targets, bucket, capacity):
    rows, width = gradients.shape
    step = 512

    def kernel(targets_ref, rows_ref, out_ref, slots_ref, pick):
        @pl.when(pl.program_id(0) == 0)
        def _():
            slots = slots_of(targets_ref[...], bucket)
            slots_ref[...] = slots
            at = lax.broadcasted_iota(jnp.int32, (capacity, rows), 0)
            pick[...] = jnp.where(at == slots, 1.0, 0.0).astype(jnp.bfloat16)

        out_ref[...] = jnp.dot(
            pick[...], rows_ref[...], preferred_element_type=jnp.float32
        ).astype(jnp.bfloat16)

    return pl.pallas_call(
        kernel,
        grid=(width // step,),
        in_specs=[
            pl.BlockSpec((1, rows), lambda i: (0, 0)),
            pl.BlockSpec((rows, step), lambda i: (0, i)),
        ],
        out_specs=[
            pl.BlockSpec((capacity, step), lambda i: (0, i)),
            pl.BlockSpec((1, rows), lambda i: (0, 0)),
        ],
        out_shape=[
            jax.ShapeDtypeStruct((capacity, width), jnp.bfloat16),
            jax.ShapeDtypeStruct((1, rows), jnp.int32),
        ],
        scratch_shapes=[pltpu.VMEM((capacity, rows), jnp.bfloat16)],
        compiler_params=pltpu.CompilerParams(vmem_limit_bytes=24 * 2**20),
        cost_estimate=pl.CostEstimate(
            flops=2 * capacity * rows * width, bytes_accessed=5 * 2**20, transcendentals=0
        ),
    )(targets, gradients)


def precondition(gradients, left, right):
    product = kron(left, gradients, right).reshape(gradients.shape)
    scale = lax.rsqrt(jnp.mean(product * product, axis=-1, keepdims=True) + 1e-06)
    return (product * scale * (1.0 / math.sqrt(product.shape[1]))).astype(jnp.bfloat16)


def reorder(blocks, order):
    outer, pairs, rows, width = blocks.shape
    deep, high, own = order
    inner = rows // deep * outer

    def kernel(in_ref, out_ref):
        total = outer * rows
        to = lax.broadcasted_iota(jnp.int32, (total, total), 0)
        source = lax.broadcasted_iota(jnp.int32, (total, total), 1)
        at_x = source // rows
        at_z = source % rows // (high * own)
        at_high = source % (high * own) // own
        goes = at_z * inner + (at_high * outer + at_x) * own + source % own
        pick = jnp.where(to == goes, 1.0, 0.0).astype(jnp.bfloat16)
        moved = jnp.dot(
            pick, in_ref[...].reshape((total, width)), preferred_element_type=jnp.float32
        )
        out_ref[...] = moved.astype(jnp.bfloat16).reshape((deep, 1, inner, width))

    return pl.pallas_call(
        kernel,
        grid=(pairs,),
        in_specs=[pl.BlockSpec((outer, 1, rows, width), lambda i: (0, i, 0, 0))],
        out_specs=pl.BlockSpec((deep, 1, inner, width), lambda i: (0, i, 0, 0)),
        out_shape=jax.ShapeDtypeStruct((deep, pairs, inner, width), jnp.bfloat16),
        compiler_params=pltpu.CompilerParams(vmem_limit_bytes=32 * 2**20),
        cost_estimate=pl.CostEstimate(
            flops=2 * pairs * (outer * rows) ** 2 * width,
            bytes_accessed=4 * pairs * outer * rows * width,
            transcendentals=0,
        ),
    )(blocks)


def body(gradients, destinations, queries, left_factor, right_factor):
    sizes = {axis: lax.axis_size(axis) for axis in STORE + PROD}
    owners = lax.axis_size(STORE)
    rows, width = gradients.shape
    bucket = 2 * rows // owners
    capacity = owners * bucket
    own = queries.shape[0]

    few = gather(queries, ("z", "y_hi")).reshape((-1, width))
    normal = precondition(gradients, left_factor, right_factor)
    buffer, slots = place(normal, destinations[None], bucket, capacity)
    few, buffer = lax.optimization_barrier((few, buffer))

    every = lax.all_gather(few, ("x", "y_lo", "core"), axis=0, tiled=True)
    every = every.reshape((sizes["x"], -1, few.shape[0], width))
    every = reorder(every, (sizes["z"], sizes["y_hi"], own)).reshape((-1, width))

    stored = exchange(buffer.reshape((owners, bucket, width)), STORE).reshape((capacity, width))
    scores = lax.dot_general(
        every, stored, (((1,), (1,)), ((), ())), preferred_element_type=jnp.float32
    )
    return scores.astype(jnp.bfloat16)


def solution(mesh):
    fine = Mesh(mesh.devices.reshape((8, 2, 2, 4, 4)), STORE + PROD)
    whole = STORE + PROD
    return jax.shard_map(
        body,
        mesh=fine,
        in_specs=(P(whole, None), P(whole), P(whole, None), P(), P()),
        out_specs=P(None, whole),
        check_vma=False,
    )
```

time: 518 us -> 154 us (0.30)
  waiting for transfers between devices: 228 us -> 73.2 us
  blocking collectives: 86.9 us -> 0 us
  matrix products: 74.3 us -> 15.7 us
  starting transfers between devices: 71 us -> 23.2 us
  local copies, waits for them, and re-layouts: 44.1 us -> 16.9 us
  between operations: 0.09 us -> 13.5 us
  Pallas kernels: 0 us -> 8.95 us
    ppermute x31 -> x0, waiting for transfers between devices: 228 us -> none  [from_behind(): return lax.ppermute(block, axis, route)]
    all_gather x1 -> x0, blocking collectives: 86.9 us -> none  [body(): local_queries = lax.all_gather(queries, 'prod', axis=0, tiled=True)]
    all_gather x0 -> x1, waiting for transfers between devices: none -> 72.6 us  [body(): every = lax.all_gather(few, ('x', 'y_lo', 'core'), axis=0, tiled=True)]
    ppermute x31 -> x0, starting transfers between devices: 59.1 us -> none  [from_behind(): return lax.ppermute(block, axis, route)]
    dot_general x34 -> x3, matrix products: 74.3 us -> 15.7 us  [the longest x1 9.21 us: body(): lax.dot_general(every, stored, (((1,), (1,)), ((), ())), preferred_elemen...]
    while x32 -> x0, local copies, waits for them, and re-layouts: 24.1 us -> none
    all_to_all x1 -> x2, starting transfers between devices: 11.9 us -> 23.2 us  [exchange(): return lax.all_to_all(block, axis, split_axis=0, concat_axis=0, tiled=True)]
    pallas_call x0 -> x2, Pallas kernels: none -> 8.95 us  [the longest x1 4.75 us: reorder(): pl.pallas_call(kernel, grid=(pairs,), in_specs=[pl.BlockSpec((outer, 1, r...]
  transfers between devices with their start and end apart: 32 -> 3, of which waited for: 31 -> 2; matrix products, arithmetic and copies ran while one was open for 0% -> 10% of each run, Pallas kernels for 0% -> 6%
where the time goes in v1:
time: 154 us; the launch traced here: 152 us
  waiting for transfers between devices  73.2 us (48%)
  starting transfers between devices  23.2 us (15%)
  local copies, waits for them, and re-layouts  16.9 us (11%)
  matrix products  15.7 us (10%)
  between operations  13.5 us (9%)
  Pallas kernels  8.95 us (6%)
    all_gather x1, waiting for transfers between devices, body(): every = lax.all_gather(few, ('x', 'y_lo', 'core'), axis=0, tiled=True)  72.6 us
    all_to_all x2, starting transfers between devices, exchange(): return lax.all_to_all(block, axis, split_axis=0, concat_axis=0, tiled=True)  23.2 us
    dot_general x1, matrix products, body(): lax.dot_general(every, stored, (((1,), (1,)), ((), ())), preferred_elemen...  9.21 us
    unnamed x11, local copies, waits for them, and re-layouts  7.33 us
    dot_general x1, matrix products, kron(): return jnp.einsum('ab,nbd->nad', left, half, precision=HIGHEST)  5 us
    pallas_call x1, Pallas kernels, reorder(): pl.pallas_call(kernel, grid=(pairs,), in_specs=[pl.BlockSpec((outer, 1, r...  4.75 us
    pallas_call x1, Pallas kernels, place(): pl.pallas_call(kernel, grid=(width // step,), in_specs=[pl.BlockSpec((1,...  4.19 us
    transpose x1, local copies, waits for them, and re-layouts, kron(): return jnp.einsum('ab,nbd->nad', left, half, precision=HIGHEST)  3.45 us
  transfers between devices with their start and end apart: 3, of which 2 were waited for; matrix products, arithmetic and copies ran while one was open for 10% of the time, Pallas kernels for 6%

profile of v1, /device:TPU:6, one launch (start us, length us, event | category | flops | bytes accessed | tf_op | source)
XLA Modules:
  0.0 151.8 jit_solution(12176858154989335770)
XLA Ops:
  6.5 1.8 %broadcast_in_dim.4 = bf16[32,3,2048]{2,1,0:T(4,128)(2,1)} broadcast(bf16[3,2048]{1,0:T(4,128)(2,1)} %param.7), dimensions={1,2} | broadcast | bytes 405504 | tf_op jit(solution)/shard_map/broadcast_in_dim | solution.py:21
  8.3 16.1 %all-to-all-start = ((bf16[32,3,2048]{2,1,0:T(4,128)(2,1)}), bf16[32,3,2048]{2,1,0:T(4,128)(2,1)}, u32[]{:S(2)}, u32[]{:S(2)}) async-start(bf16[32,3,2048]{2,1,0:T(4,128)(2,1)} %broadcast_in_dim.4), calls=%async_computation | async-start | bytes 1048576 | tf_op jit(solution)/shard_map/all_to_all | solution.py:16
  24.4 0.0 all-gather.2.cloned.1.call-start
  24.4 1.9 %copy.7 = bf16[384,2048]{0,1:T(8,128)(2,1)S(1)} copy(bf16[384,2048]{1,0:T(8,128)(2,1)} %param.5) | data formatting | bytes 3145728 | tf_op args[0]
  26.3 0.0 copy-start.3
  26.4 1.5 fusion.5
  27.8 0.0 copy-done.3
  27.8 0.0 copy-start.4
  27.9 5.0 %multiply_reduce_fusion = (f32[384]{0:T(512)S(1)}, f32[384,32,64]{0,1,2:T(8,128)S(1)}) fusion(f32[32,32]{1,0:T(8,128)S(1)} %copy-done.3, f32[384,32,64]{0,2,1:T(8,128)S(1)} %fusion.5), kind=kOutput, calls=%fused_computation.4 | convolution fusion | flops 303562368 | bytes 6297088 | tf_op jit(solution)/shard_map/ab,nbd->nad/dot_general | solution.py:28
  32.9 0.0 copy-done.4
  32.9 3.4 %copy.8 = f32[384,32,64]{0,2,1:T(8,128)} copy(f32[384,32,64]{0,1,2:T(8,128)S(1)} %get-tuple-element.12) | data formatting | bytes 6291456 | tf_op jit(solution)/shard_map/ab,nbd->nad/transpose | solution.py:28
  36.3 2.4 %copy.9 = f32[384,2048]{1,0:T(8,128)S(1)} copy(f32[384,2048]{0,1:T(8,128)} %bitcast.21) | data formatting | bytes 6291456 | tf_op jit(solution)/shard_map/reshape | solution.py:80
  38.7 0.3 multiply_convert_fusion.rows_ref
  39.0 4.2 %shard_map.55 = (bf16[768,2048]{1,0:T(8,128)(2,1)}, s32[1,384]{1,0:T(1,128)}) custom-call(s32[1,384]{1,0:T(1,128)S(1)} %broadcast_in_dim.5.targets_ref, bf16[384,2048]{1,0:T(8,128)(2,1)S(1)} %multiply_convert_fusion.rows_ref), custom_call_target="tpu_custom_call" | custom-call | flops 1207959552 | bytes 5242880 | tf_op jit(solution)/shard_map/pallas_call | solution.py:56
  43.2 0.5 all-to-all-done
  43.8 2.0 %reshape.30 = bf16[96,2048]{1,0:T(8,128)(2,1)} reshape(bf16[32,3,2048]{2,1,0:T(4,128)(2,1)} %all-to-all-done) | data formatting | bytes 786432 | tf_op jit(solution)/shard_map/reshape | solution.py:127
  45.8 0.0 all-gather.2.cloned.1.call-update
  45.8 7.1 %all-to-all-start.1 = ((bf16[32,24,2048]{2,1,0:T(8,128)(2,1)}), bf16[32,24,2048]{2,1,0:T(8,128)(2,1)S(1)}, u32[]{:S(2)}, u32[]{:S(2)}) async-start(bf16[32,24,2048]{2,1,0:T(8,128)(2,1)} %bitcast.7), calls=%async_computation.1 | async-start | bytes 6291456 | tf_op jit(solution)/shard_map/all_to_all | solution.py:16
  52.9 72.6 %all-gather.2.cloned.1.call-done = bf16[1536,2048]{1,0:T(8,128)(2,1)} async-done(((bf16[96,2048]{1,0:T(8,128)(2,1)}), bf16[1536,2048]{1,0:T(8,128)(2,1)}) %all-gather.2.cloned.1.call-update) | async-done | bytes 6291472 | tf_op jit(solution)/shard_map/all_gather | solution.py:132
  125.5 2.8 %copy-done.1 = bf16[1536,2048]{1,0:T(8,128)(2,1)S(1)} copy-done((bf16[1536,2048]{1,0:T(8,128)(2,1)S(1)}, bf16[1536,2048]{1,0:T(8,128)(2,1)}, u32[]{:S(2)}) %copy-start.1) | copy-done | bytes 6291480
  128.3 4.8 %shard_map.56 = bf16[8,4,48,2048]{3,2,1,0:T(8,128)(2,1)S(1)} custom-call(bf16[4,4,96,2048]{3,2,1,0:T(8,128)(2,1)S(1)} %bitcast.19), custom_call_target="tpu_custom_call" | custom-call | flops 2415919104 | bytes 12582912 | tf_op jit(solution)/shard_map/pallas_call | solution.py:104
  133.1 2.6 %copy-done.2 = bf16[8,4,48,2048]{3,2,1,0:T(8,128)(2,1)} copy-done((bf16[8,4,48,2048]{3,2,1,0:T(8,128)(2,1)}, bf16[8,4,48,2048]{3,2,1,0:T(8,128)(2,1)S(1)}, u32[]{:S(2)}) %copy-start.2) | copy-done | bytes 6291480
  135.7 0.0 all-to-all-done.1
  135.7 9.2 %convolution_convert_fusion = bf16[1536,768]{1,0:T(8,128)(2,1)} fusion(bf16[1536,2048]{1,0:T(8,128)(2,1)} %bitcast.20, bf16[768,2048]{1,0:T(8,128)(2,1)S(1)} %bitcast.23), kind=kOutput, calls=%fused_computation | convolution fusion | flops 4833017856 | bytes 11796480 | tf_op jit(solution)/shard_map/dot_general | solution.py:137
  (6 shorter events, 0.0 us)
Async XLA Ops:
  6.5 19.8 %copy-start = (f32[64,64]{1,0:T(8,128)S(1)}, f32[64,64]{1,0:T(8,128)}, u32[]{:S(2)}) copy-start(f32[64,64]{1,0:T(8,128)} %param.9) | copy-start | bytes 49156
  8.3 35.5 %all-to-all-start = ((bf16[32,3,2048]{2,1,0:T(4,128)(2,1)}), bf16[32,3,2048]{2,1,0:T(4,128)(2,1)}, u32[]{:S(2)}, u32[]{:S(2)}) async-start(bf16[32,3,2048]{2,1,0:T(4,128)(2,1)} %broadcast_in_dim.4), calls=%async_computation | async-start | bytes 1048576 | tf_op jit(solution)/shard_map/all_to_all | solution.py:16
  24.4 101.1 %all-gather.2.cloned.1.call-start = ((), (), s32[]{:S(2)}) async-start(), calls=%async_computation.2 | async-start | bytes 6684672 | tf_op jit(solution)/shard_map/all_gather | solution.py:132
  26.3 1.5 copy-start.3
  27.8 5.0 %copy-start.4 = (s32[384]{0:T(512)S(1)}, s32[384]{0:T(512)}, u32[]{:S(2)}) copy-start(s32[384]{0:T(512)} %param.6) | copy-start | bytes 4612
  45.8 89.9 %all-to-all-start.1 = ((bf16[32,24,2048]{2,1,0:T(8,128)(2,1)}), bf16[32,24,2048]{2,1,0:T(8,128)(2,1)S(1)}, u32[]{:S(2)}, u32[]{:S(2)}) async-start(bf16[32,24,2048]{2,1,0:T(8,128)(2,1)} %bitcast.7), calls=%async_computation.1 | async-start | bytes 6291456 | tf_op jit(solution)/shard_map/all_to_all | solution.py:16
  125.5 2.8 %copy-start.1 = (bf16[1536,2048]{1,0:T(8,128)(2,1)S(1)}, bf16[1536,2048]{1,0:T(8,128)(2,1)}, u32[]{:S(2)}) copy-start(bf16[1536,2048]{1,0:T(8,128)(2,1)} %all-gather.2.cloned.1.call-done) | copy-start | bytes 18874372
  133.1 2.7 %copy-start.2 = (bf16[8,4,48,2048]{3,2,1,0:T(8,128)(2,1)}, bf16[8,4,48,2048]{3,2,1,0:T(8,128)(2,1)S(1)}, u32[]{:S(2)}) copy-start(bf16[8,4,48,2048]{3,2,1,0:T(8,128)(2,1)S(1)} %shard_map.56) | copy-start | bytes 18874372
Sparse Core Ops, SparseCore 0:
  45.9 79.5 all-gather.1

commit v2 on v1

v2 whole, which is shorter than its diff:
```python
import math

import jax
import jax.numpy as jnp
from jax import lax
from jax.experimental import pallas as pl
from jax.experimental.pallas import tpu as pltpu
from jax.sharding import Mesh, PartitionSpec as P

STORE = ("z", "y_lo", "core")
PROD = ("y_hi", "x")
VMEM = pl.BlockSpec(memory_space=pltpu.VMEM)


def exchange(block, axis):
    return lax.all_to_all(block, axis, split_axis=0, concat_axis=0, tiled=True)


def gather(block, axis):
    count = lax.axis_size(axis)
    return exchange(jnp.broadcast_to(block[None], (count,) + block.shape), axis)


def shift(block, axis, by):
    count = lax.axis_size(axis)
    return lax.ppermute(block, axis, [(i, (i + by) % count) for i in range(count)])


def slots_of(targets, bucket):
    rows = targets.shape[1]
    above = lax.broadcasted_iota(jnp.int32, (rows, rows), 0)
    along = lax.broadcasted_iota(jnp.int32, (rows, rows), 1)
    upright = jnp.sum(jnp.where(above == along, targets, 0), axis=1, keepdims=True)
    earlier = jnp.where((upright == targets) & (above < along), 1, 0)
    return targets * bucket + jnp.sum(earlier, axis=0, keepdims=True)


def prepare(gradients, targets, left, right, bucket, capacity, step=512):
    rows, width = gradients.shape
    deep, fine = left.shape[1], right.shape[0]
    steps = width // step
    spread = jnp.repeat(left.T, fine, axis=1)
    tiled = jnp.tile(right, (1, step // fine))

    def kernel(targets_ref, rows_ref, spread_ref, tiled_ref, out_ref, product, squares, pick):
        i = pl.program_id(0)

        @pl.when(i == 0)
        def _():
            squares[...] = jnp.zeros_like(squares)

        @pl.when(i < steps)
        def _():
            factor = spread_ref[...][:, None, :] * tiled_ref[...][None]
            factor = factor.reshape((width, step))
            high = factor.astype(jnp.bfloat16)
            low = (factor - high.astype(jnp.float32)).astype(jnp.bfloat16)
            part = jnp.dot(rows_ref[...], high, preferred_element_type=jnp.float32)
            part = part + jnp.dot(rows_ref[...], low, preferred_element_type=jnp.float32)
            product[i] = part
            squares[...] += jnp.sum(part * part, axis=1, keepdims=True)

        @pl.when(i == steps)
        def _():
            slots = slots_of(targets_ref[...], bucket)
            at = lax.broadcasted_iota(jnp.int32, (capacity, rows), 0)
            pick[...] = jnp.where(at == slots, 1.0, 0.0).astype(jnp.bfloat16)
            squares[...] = lax.rsqrt(squares[...] / width + 1e-06) * (1.0 / math.sqrt(width))

        @pl.when(i >= steps)
        def _():
            normal = (product[i - steps] * squares[...]).astype(jnp.bfloat16)
            out_ref[...] = jnp.dot(
                pick[...], normal, preferred_element_type=jnp.float32
            ).astype(jnp.bfloat16)

    return pl.pallas_call(
        kernel,
        grid=(2 * steps,),
        in_specs=[
            pl.BlockSpec((1, rows), lambda i: (0, 0)),
            pl.BlockSpec((rows, width), lambda i: (0, 0)),
            pl.BlockSpec((deep, step), lambda i: (0, jnp.minimum(i, steps - 1))),
            pl.BlockSpec((fine, step), lambda i: (0, 0)),
        ],
        out_specs=pl.BlockSpec((capacity, step), lambda i: (0, jnp.maximum(i - steps, 0))),
        out_shape=jax.ShapeDtypeStruct((capacity, width), jnp.bfloat16),
        scratch_shapes=[
            pltpu.VMEM((steps, rows, step), jnp.float32),
            pltpu.VMEM((rows, 1), jnp.float32),
            pltpu.VMEM((capacity, rows), jnp.bfloat16),
        ],
        compiler_params=pltpu.CompilerParams(vmem_limit_bytes=60 * 2**20),
        cost_estimate=pl.CostEstimate(
            flops=2 * rows * width * (2 * width + capacity),
            bytes_accessed=6 * 2**20,
            transcendentals=0,
        ),
    )(targets, gradients, spread, tiled)


def reorder(place_of, pair, before, after, far, order):
    deep, high, own = order
    flips, rows, width = pair.shape
    outer = lax.axis_size("x")
    inner = high * outer * own
    total = outer * rows

    def kernel(at_ref, pair_ref, before_ref, after_ref, far0_ref, far1_ref, out_ref, held, sems):
        copies = []
        for flip, far_ref in enumerate((far0_ref, far1_ref)):
            sources = [ref.at[flip] for ref in (pair_ref, before_ref, after_ref)] + [far_ref]
            for s, source_ref in enumerate(sources):
                there = held.at[flip, pl.ds(s * rows, rows)]
                copies.append(pltpu.make_async_copy(source_ref, there, sems.at[flip, s]))
        for copy in copies:
            copy.start()
        to = lax.broadcasted_iota(jnp.int32, (total, total), 0)
        source = lax.broadcasted_iota(jnp.int32, (total, total), 1)
        slot = source // rows
        move = jnp.where(slot == 1, outer - 1, jnp.where(slot == 2, 1, jnp.where(slot == 3, 2, 0)))
        at_x = (at_ref[0] + move) % outer
        at_z = source % rows // (high * own)
        at_high = source % (high * own) // own
        goes = at_z * inner + (at_high * outer + at_x) * own + source % own
        pick = jnp.where(to == goes, 1.0, 0.0).astype(jnp.bfloat16)
        for copy in copies:
            copy.wait()
        for flip in range(flips):
            moved = jnp.dot(pick, held[flip], preferred_element_type=jnp.float32)
            where = (at_ref[1] + flip) % flips
            out_ref[:, pl.ds(where, 1)] = moved.astype(jnp.bfloat16).reshape((deep, 1, inner, width))

    hbm = pl.BlockSpec(memory_space=pltpu.HBM)
    return pl.pallas_call(
        kernel,
        in_specs=[pl.BlockSpec(memory_space=pltpu.SMEM)] + [hbm] * 5,
        out_specs=VMEM,
        out_shape=jax.ShapeDtypeStruct((deep, flips, inner, width), jnp.bfloat16),
        scratch_shapes=[
            pltpu.VMEM((flips, total, width), jnp.bfloat16),
            pltpu.SemaphoreType.DMA((flips, outer)),
        ],
        compiler_params=pltpu.CompilerParams(vmem_limit_bytes=60 * 2**20),
        cost_estimate=pl.CostEstimate(
            flops=6 * flips * total * total * width,
            bytes_accessed=4 * flips * total * width,
            transcendentals=0,
        ),
    )(place_of, pair, before, after, *far)


def score(place_of, own_core, other_core, stored):
    deep, flips, inner, width = own_core.shape
    capacity = stored.shape[0]
    blocks = deep * flips
    half, wide = blocks // 2, capacity // 2

    def kernel(at_ref, own_ref, other_ref, stored_ref, out_ref, held, kept, sems):
        i = pl.program_id(0)
        queries = [
            pltpu.make_async_copy(
                (own_ref, other_ref)[j // 2].at[pl.ds(j % 2 * half, half)], held.at[j], sems.at[j]
            )
            for j in range(4)
        ]
        columns = [
            pltpu.make_async_copy(stored_ref.at[pl.ds(h * wide, wide)], kept.at[h], sems.at[4 + h])
            for h in range(2)
        ]

        @pl.when(i == 0)
        def _():
            for copy in (queries[0], columns[0], columns[1], *queries[1:]):
                copy.start()

        for j in range(4):
            for h in range(2):

                @pl.when(i == 2 * j + h)
                def _():
                    if h == 0:
                        queries[j].wait()
                    if j == 0:
                        columns[h].wait()
                    scores = lax.dot_general(
                        held[j].reshape((half * inner, width)),
                        kept[h],
                        (((1,), (1,)), ((), ())),
                        preferred_element_type=jnp.float32,
                    )
                    scores = scores.astype(jnp.bfloat16).reshape((half, 1, inner, wide))
                    out_ref[:, :, :, h * wide : (h + 1) * wide] = scores

    hbm = pl.BlockSpec(memory_space=pltpu.HBM)
    out = pl.pallas_call(
        kernel,
        grid_spec=pltpu.PrefetchScalarGridSpec(
            num_scalar_prefetch=1,
            grid=(8,),
            in_specs=[hbm, hbm, hbm],
            out_specs=pl.BlockSpec(
                (half, 1, inner, capacity), lambda i, at: (i // 2 % 2, (at[2] + i // 4) % 2, 0, 0)
            ),
            scratch_shapes=[
                pltpu.VMEM((4, half, inner, width), jnp.bfloat16),
                pltpu.VMEM((2, wide, width), jnp.bfloat16),
                pltpu.SemaphoreType.DMA((6,)),
            ],
        ),
        out_shape=jax.ShapeDtypeStruct((blocks, 2, inner, capacity), jnp.bfloat16),
        compiler_params=pltpu.CompilerParams(vmem_limit_bytes=60 * 2**20),
        cost_estimate=pl.CostEstimate(
            flops=4 * blocks * inner * capacity * width,
            bytes_accessed=12 * 2**20,
            transcendentals=0,
        ),
    )(place_of, *(a.reshape((blocks, inner, width)) for a in (own_core, other_core)), stored)
    return out.reshape((-1, capacity))


def body(gradients, destinations, queries, left_factor, right_factor):
    owners = lax.axis_size(STORE)
    rows, width = gradients.shape
    bucket = 2 * rows // owners
    capacity = owners * bucket
    own = queries.shape[0]
    order = (lax.axis_size("z"), lax.axis_size("y_hi"), own)

    line = gather(queries.reshape((-1, 128)), ("z", "y_hi"))
    buffer = prepare(gradients, destinations[None], left_factor, right_factor, bucket, capacity)
    line, buffer = lax.optimization_barrier((line, buffer))
    near = shift(line, "y_lo", 1)
    stored = exchange(buffer.reshape((owners, bucket, width)), STORE).reshape((capacity, width))

    pair = jnp.stack([line, near]).reshape((2, -1, width))
    before, after = shift(pair, "x", 1), shift(pair, "x", -1)
    far = (shift(before[0], "x", 1), shift(after[1], "x", -1))
    place_of = jnp.stack([lax.axis_index(a) for a in ("x", "y_lo", "core")]).astype(jnp.int32)
    mine = reorder(place_of, pair, before, after, far, order)
    others = shift(mine, "core", 1)
    return score(place_of, mine, others, stored)


def solution(mesh):
    fine = Mesh(mesh.devices.reshape((8, 2, 2, 4, 4)), STORE + PROD)
    whole = STORE + PROD
    return jax.shard_map(
        body,
        mesh=fine,
        in_specs=(P(whole, None), P(whole), P(whole, None), P(), P()),
        out_specs=P(None, whole),
        check_vma=False,
    )
```

time: 154 us -> 144 us (0.935); the launches traced: 152 us -> 143 us
  Pallas kernels: 8.95 us -> 31.7 us
  starting transfers between devices: 23.2 us -> 42.9 us
  waiting for transfers between devices: 73.2 us -> 53.6 us
  matrix products: 15.7 us -> 0 us
  between operations: 13.5 us -> 0.29 us
  local copies, waits for them, and re-layouts: 16.9 us -> 14.2 us
    all_gather x1 -> x0, waiting for transfers between devices: 72.6 us -> none  [body(): every = lax.all_gather(few, ('x', 'y_lo', 'core'), axis=0, tiled=True)]
    ppermute x0 -> x6, waiting for transfers between devices: none -> 29.2 us  [shift(): lax.ppermute(block, axis, [(i, (i + by) % count) for i in range(count)])]
    all_to_all x2, waiting for transfers between devices: 0.55 us -> 24.5 us  [exchange(): return lax.all_to_all(block, axis, split_axis=0, concat_axis=0, tiled=True)]
    pallas_call x2 -> x3, Pallas kernels: 8.95 us -> 31.7 us  [the longest x1 13.7 us: prepare(): pl.pallas_call(kernel, grid=(2 * steps,), in_specs=[pl.BlockSpec((1, rows...]
    ppermute x0 -> x6, starting transfers between devices: none -> 18.8 us  [shift(): lax.ppermute(block, axis, [(i, (i + by) % count) for i in range(count)])]
    dot_general x3 -> x0, matrix products: 15.7 us -> none  [the longest x1 9.21 us: body(): lax.dot_general(every, stored, (((1,), (1,)), ((), ())), preferred_elemen...]
    another operation x0 -> x5, local copies, waits for them, and re-layouts: none -> 4.42 us  [the longest x3 2.88 us: body(): pair = jnp.stack([line, near]).reshape((2, -1, width))]
    reshape x2 -> x1, local copies, waits for them, and re-layouts: 4.39 us -> 0.9 us  [prepare(): spread = jnp.repeat(left.T, fine, axis=1)]
  transfers between devices with their start and end apart: 3 -> 8, of which waited for: 2 -> 5; matrix products, arithmetic and copies ran while one was open for 10% -> 7% of each run, Pallas kernels for 6% -> 14%
where the time goes in v2:
time: 144 us; the launch traced here: 143 us
  waiting for transfers between devices  53.6 us (37%)
  starting transfers between devices  42.9 us (30%)
  Pallas kernels  31.7 us (22%)
  local copies, waits for them, and re-layouts  14.2 us (10%)
    ppermute x6, waiting for transfers between devices, shift(): lax.ppermute(block, axis, [(i, (i + by) % count) for i in range(count)])  29.2 us
    all_to_all x2, waiting for transfers between devices, exchange(): return lax.all_to_all(block, axis, split_axis=0, concat_axis=0, tiled=True)  24.5 us
    all_to_all x2, starting transfers between devices, exchange(): return lax.all_to_all(block, axis, split_axis=0, concat_axis=0, tiled=True)  24.1 us
    ppermute x6, starting transfers between devices, shift(): lax.ppermute(block, axis, [(i, (i + by) % count) for i in range(count)])  18.8 us
    pallas_call x1, Pallas kernels, prepare(): pl.pallas_call(kernel, grid=(2 * steps,), in_specs=[pl.BlockSpec((1, rows...  13.7 us
    pallas_call x1, Pallas kernels, score(): pl.pallas_call(kernel, grid_spec=pltpu.PrefetchScalarGridSpec(num_scalar_...  12 us
    pallas_call x1, Pallas kernels, reorder(): pl.pallas_call(kernel, in_specs=[pl.BlockSpec(memory_space=pltpu.SMEM)] +...  6.02 us
    unnamed x7, local copies, waits for them, and re-layouts  4.29 us
  transfers between devices with their start and end apart: 8, of which 5 were waited for; matrix products, arithmetic and copies ran while one was open for 7% of the time, Pallas kernels for 14%

profile of v2, /device:TPU:6, one launch (start us, length us, event | category | flops | bytes accessed | tf_op | source)
XLA Modules:
  0.0 143.4 jit_solution(3276555470795845319)
XLA Ops:
  0.7 0.8 broadcast_in_dim.14
  1.5 16.0 %all-to-all-start = ((bf16[32,48,128]{2,1,0:T(8,128)(2,1)}), bf16[32,48,128]{2,1,0:T(8,128)(2,1)S(1)}, u32[]{:S(2)}, u32[]{:S(2)}) async-start(bf16[32,48,128]{2,1,0:T(8,128)(2,1)} %broadcast_in_dim.14), calls=%async_computation | async-start | bytes 786432 | tf_op jit(solution)/shard_map/all_to_all | solution.py:16
  17.5 1.3 broadcast_in_dim.15.targets_ref
  21.3 0.9 reshape.28.spread_ref
  22.2 13.7 %shard_map.55 = bf16[768,2048]{1,0:T(8,128)(2,1)} custom-call(s32[1,384]{1,0:T(1,128)} %broadcast_in_dim.15.targets_ref, bf16[384,2048]{1,0:T(8,128)(2,1)} %rows_ref.1, f32[32,2048]{1,0:T(8,128)} %reshape.28.spread_ref, f32[64,512]{1,0:T(8,128)} %tile.10.tiled_ref), custom_call_target="tpu_custom_call" | custom-call | flops 7650410496 | bytes 6291456 | tf_op jit(solution)/shard_map/pallas_call | solution.py:77
  35.9 2.6 %collective-permute-start = (bf16[32,48,128]{2,1,0:T(8,128)(2,1)S(1)}, bf16[32,48,128]{2,1,0:T(8,128)(2,1)}, u32[]{:S(2)}, u32[]{:S(2)}) collective-permute-start(bf16[32,48,128]{2,1,0:T(8,128)(2,1)S(1)} %all-to-all-done), channel_id=1, source_target_pairs={{0,32},{32,0},{1,33},{33,1},{2,34},{34,2},{3,35},{35,3},{4,36},{36... | collective-permute-start | bytes 1179656 | tf_op jit(solution)/shard_map/ppermute | solution.py:26
  38.5 8.2 %all-to-all-start.1 = ((bf16[32,24,2048]{2,1,0:T(8,128)(2,1)}), bf16[32,24,2048]{2,1,0:T(8,128)(2,1)S(1)}, u32[]{:S(2)}, u32[]{:S(2)}) async-start(bf16[32,24,2048]{2,1,0:T(8,128)(2,1)} %bitcast.13), calls=%async_computation.1 | async-start | bytes 6291456 | tf_op jit(solution)/shard_map/all_to_all | solution.py:16
  46.7 0.9 stack.25
  47.6 1.8 %constant_dynamic-update-slice_fusion.1 = bf16[2,96,2048]{2,1,0:T(8,128)(2,1)} fusion(bf16[1,96,2048]{2,1,0:T(8,128)(2,1)} %stack.25), kind=kLoop, calls=%fused_computation.3 | loop fusion | bytes 786432
  49.4 1.2 stack.26
  51.3 2.7 %collective-permute-start.2 = (bf16[2,96,2048]{2,1,0:T(8,128)(2,1)}, bf16[2,96,2048]{2,1,0:T(8,128)(2,1)S(1)}, u32[]{:S(2)}, u32[]{:S(2)}) collective-permute-start(bf16[2,96,2048]{2,1,0:T(8,128)(2,1)} %constant_dynamic-update-slice_fusion.pair_ref), channel_id=1, source_target_pairs={{0,3},{1,0},{2,1},{3,2},{4,7},{5,4},{6,5},{7,6},{8,11},{9,8},{10,9... | collective-permute-start | bytes 2359304 | tf_op jit(solution)/shard_map/ppermute | solution.py:26
  54.1 4.3 %collective-permute-start.1 = (bf16[2,96,2048]{2,1,0:T(8,128)(2,1)}, bf16[2,96,2048]{2,1,0:T(8,128)(2,1)S(1)}, u32[]{:S(2)}, u32[]{:S(2)}) collective-permute-start(bf16[2,96,2048]{2,1,0:T(8,128)(2,1)} %constant_dynamic-update-slice_fusion.pair_ref), channel_id=1, source_target_pairs={{0,1},{1,2},{2,3},{3,0},{4,5},{5,6},{6,7},{7,4},{8,9},{9,10},{10,1... | collective-permute-start | bytes 2359304 | tf_op jit(solution)/shard_map/ppermute | solution.py:26
  58.4 16.0 %collective-permute-done.2.after_ref = bf16[2,96,2048]{2,1,0:T(8,128)(2,1)S(1)} collective-permute-done((bf16[2,96,2048]{2,1,0:T(8,128)(2,1)}, bf16[2,96,2048]{2,1,0:T(8,128)(2,1)S(1)}, u32[]{:S(2)}, u32[]{:S(2)}) %collective-permute-start.2) | collective-permute-done | bytes 786464 | tf_op jit(solution)/shard_map/ppermute | solution.py:26
  74.4 1.9 %collective-permute-start.4 = (bf16[96,2048]{1,0:T(8,128)(2,1)S(1)}, bf16[96,2048]{1,0:T(8,128)(2,1)}, u32[]{:S(2)}, u32[]{:S(2)}) collective-permute-start(bf16[96,2048]{1,0:T(8,128)(2,1)S(1)} %slice_bitcast_fusion), channel_id=1, source_target_pairs={{0,3},{1,0},{2,1},{3,2},{4,7},{5,4},{6,5},{7,6},{8,11},{9,8},{10,9... | collective-permute-start | bytes 1179656 | tf_op jit(solution)/shard_map/ppermute | solution.py:26
  76.4 0.9 copy-done.2
  78.0 5.1 %collective-permute-start.3 = (bf16[96,2048]{1,0:T(8,128)(2,1)}, bf16[96,2048]{1,0:T(8,128)(2,1)}, u32[]{:S(2)}, u32[]{:S(2)}) collective-permute-start(bf16[96,2048]{1,0:T(8,128)(2,1)} %slice_bitcast_fusion.1), channel_id=1, source_target_pairs={{0,1},{1,2},{2,3},{3,0},{4,5},{5,6},{6,7},{7,4},{8,9},{9,10},{10,1... | collective-permute-start | bytes 1179656 | tf_op jit(solution)/shard_map/ppermute | solution.py:26
  83.8 4.3 %collective-permute-done.4.far1_ref = bf16[96,2048]{1,0:T(8,128)(2,1)} collective-permute-done((bf16[96,2048]{1,0:T(8,128)(2,1)S(1)}, bf16[96,2048]{1,0:T(8,128)(2,1)}, u32[]{:S(2)}, u32[]{:S(2)}) %collective-permute-start.4) | collective-permute-done | bytes 393248 | tf_op jit(solution)/shard_map/ppermute | solution.py:26
  88.1 3.1 %collective-permute-done.3.far0_ref = bf16[96,2048]{1,0:T(8,128)(2,1)} collective-permute-done((bf16[96,2048]{1,0:T(8,128)(2,1)}, bf16[96,2048]{1,0:T(8,128)(2,1)}, u32[]{:S(2)}, u32[]{:S(2)}) %collective-permute-start.3) | collective-permute-done | bytes 393248 | tf_op jit(solution)/shard_map/ppermute | solution.py:26
  91.2 6.0 %shard_map.56 = bf16[8,2,48,2048]{3,2,1,0:T(8,128)(2,1)} custom-call(s32[3]{0:T(128)} %pad_add_fusion.at_ref, bf16[2,96,2048]{2,1,0:T(8,128)(2,1)} %constant_dynamic-update-slice_fusion.pair_ref, bf16[2,96,2048]{2,1,0:T(8,128)(2,1)} %copy-done.2, bf16[2,96,2048]{2,1,0:T(8,128)(2,1)} %copy-done.1, bf16[96,2048]{1,0:T(8,128)(2,1)} %collective-permute-done.3.far0_ref, ...), custom_call_target="tpu_custom_call" | custom-call | flops 3623878656 | bytes 6291456 | tf_op jit(solution)/shard_map/pallas_call | solution.py:135
  97.2 2.1 %collective-permute-start.5 = (bf16[8,2,48,2048]{3,2,1,0:T(8,128)(2,1)}, bf16[8,2,48,2048]{3,2,1,0:T(8,128)(2,1)}, u32[]{:S(2)}, u32[]{:S(2)}) collective-permute-start(bf16[8,2,48,2048]{3,2,1,0:T(8,128)(2,1)} %shard_map.56), channel_id=1, source_target_pairs={{0,16},{16,0},{1,17},{17,1},{2,18},{18,2},{3,19},{19,3},{4,20},{20... | collective-permute-start | bytes 9437192 | tf_op jit(solution)/shard_map/ppermute | solution.py:26
  99.3 5.8 %collective-permute-done.5 = bf16[8,2,48,2048]{3,2,1,0:T(8,128)(2,1)} collective-permute-done((bf16[8,2,48,2048]{3,2,1,0:T(8,128)(2,1)}, bf16[8,2,48,2048]{3,2,1,0:T(8,128)(2,1)}, u32[]{:S(2)}, u32[]{:S(2)}) %collective-permute-start.5) | collective-permute-done | bytes 3145760 | tf_op jit(solution)/shard_map/ppermute | solution.py:26
  105.1 24.5 %all-to-all-done.1 = bf16[32,24,2048]{2,1,0:T(8,128)(2,1)S(1)} async-done(((bf16[32,24,2048]{2,1,0:T(8,128)(2,1)}), bf16[32,24,2048]{2,1,0:T(8,128)(2,1)S(1)}, u32[]{:S(2)}, u32[]{:S(2)}) %all-to-all-start.1) | async-done | bytes 3145760 | tf_op jit(solution)/shard_map/all_to_all | solution.py:16
  129.6 1.6 %copy-done = bf16[32,24,2048]{2,1,0:T(8,128)(2,1)} copy-done((bf16[32,24,2048]{2,1,0:T(8,128)(2,1)}, bf16[32,24,2048]{2,1,0:T(8,128)(2,1)S(1)}, u32[]{:S(2)}) %copy-start) | copy-done | bytes 3145752
  131.2 12.0 %shard_map.57 = bf16[16,2,48,768]{3,2,1,0:T(8,128)(2,1)} custom-call(s32[3]{0:T(128)} %pad_add_fusion.at_ref, bf16[16,48,2048]{2,1,0:T(8,128)(2,1)} %bitcast.16, bf16[16,48,2048]{2,1,0:T(8,128)(2,1)} %bitcast.7.other_ref, bf16[768,2048]{1,0:T(8,128)(2,1)} %bitcast.14), custom_call_target="tpu_custom_call" | custom-call | flops 4831838208 | bytes 12582912 | tf_op jit(solution)/shard_map/pallas_call | solution.py:196
  (16 shorter events, 5.5 us)
Async XLA Ops:
  1.5 34.4 %all-to-all-start = ((bf16[32,48,128]{2,1,0:T(8,128)(2,1)}), bf16[32,48,128]{2,1,0:T(8,128)(2,1)S(1)}, u32[]{:S(2)}, u32[]{:S(2)}) async-start(bf16[32,48,128]{2,1,0:T(8,128)(2,1)} %broadcast_in_dim.14), calls=%async_computation | async-start | bytes 786432 | tf_op jit(solution)/shard_map/all_to_all | solution.py:16
  35.9 13.5 %collective-permute-start = (bf16[32,48,128]{2,1,0:T(8,128)(2,1)S(1)}, bf16[32,48,128]{2,1,0:T(8,128)(2,1)}, u32[]{:S(2)}, u32[]{:S(2)}) collective-permute-start(bf16[32,48,128]{2,1,0:T(8,128)(2,1)S(1)} %all-to-all-done), channel_id=1, source_target_pairs={{0,32},{32,0},{1,33},{33,1},{2,34},{34,2},{3,35},{35,3},{4,36},{36... | collective-permute-start | bytes 1179656 | tf_op jit(solution)/shard_map/ppermute | solution.py:26
  38.5 91.0 %all-to-all-start.1 = ((bf16[32,24,2048]{2,1,0:T(8,128)(2,1)}), bf16[32,24,2048]{2,1,0:T(8,128)(2,1)S(1)}, u32[]{:S(2)}, u32[]{:S(2)}) async-start(bf16[32,24,2048]{2,1,0:T(8,128)(2,1)} %bitcast.13), calls=%async_computation.1 | async-start | bytes 6291456 | tf_op jit(solution)/shard_map/all_to_all | solution.py:16
  51.3 23.0 %collective-permute-start.2 = (bf16[2,96,2048]{2,1,0:T(8,128)(2,1)}, bf16[2,96,2048]{2,1,0:T(8,128)(2,1)S(1)}, u32[]{:S(2)}, u32[]{:S(2)}) collective-permute-start(bf16[2,96,2048]{2,1,0:T(8,128)(2,1)} %constant_dynamic-update-slice_fusion.pair_ref), channel_id=1, source_target_pairs={{0,3},{1,0},{2,1},{3,2},{4,7},{5,4},{6,5},{7,6},{8,11},{9,8},{10,9... | collective-permute-start | bytes 2359304 | tf_op jit(solution)/shard_map/ppermute | solution.py:26
  54.1 22.3 %collective-permute-start.1 = (bf16[2,96,2048]{2,1,0:T(8,128)(2,1)}, bf16[2,96,2048]{2,1,0:T(8,128)(2,1)S(1)}, u32[]{:S(2)}, u32[]{:S(2)}) collective-permute-start(bf16[2,96,2048]{2,1,0:T(8,128)(2,1)} %constant_dynamic-update-slice_fusion.pair_ref), channel_id=1, source_target_pairs={{0,1},{1,2},{2,3},{3,0},{4,5},{5,6},{6,7},{7,4},{8,9},{9,10},{10,1... | collective-permute-start | bytes 2359304 | tf_op jit(solution)/shard_map/ppermute | solution.py:26
  74.4 2.0 %copy-start.1 = (bf16[2,96,2048]{2,1,0:T(8,128)(2,1)}, bf16[2,96,2048]{2,1,0:T(8,128)(2,1)S(1)}, u32[]{:S(2)}) copy-start(bf16[2,96,2048]{2,1,0:T(8,128)(2,1)S(1)} %collective-permute-done.2.after_ref) | copy-start | bytes 2359300
  74.4 13.7 %collective-permute-start.4 = (bf16[96,2048]{1,0:T(8,128)(2,1)S(1)}, bf16[96,2048]{1,0:T(8,128)(2,1)}, u32[]{:S(2)}, u32[]{:S(2)}) collective-permute-start(bf16[96,2048]{1,0:T(8,128)(2,1)S(1)} %slice_bitcast_fusion), channel_id=1, source_target_pairs={{0,3},{1,0},{2,1},{3,2},{4,7},{5,4},{6,5},{7,6},{8,11},{9,8},{10,9... | collective-permute-start | bytes 1179656 | tf_op jit(solution)/shard_map/ppermute | solution.py:26
  76.4 0.9 copy-start.2
  78.0 13.1 %collective-permute-start.3 = (bf16[96,2048]{1,0:T(8,128)(2,1)}, bf16[96,2048]{1,0:T(8,128)(2,1)}, u32[]{:S(2)}, u32[]{:S(2)}) collective-permute-start(bf16[96,2048]{1,0:T(8,128)(2,1)} %slice_bitcast_fusion.1), channel_id=1, source_target_pairs={{0,1},{1,2},{2,3},{3,0},{4,5},{5,6},{6,7},{7,4},{8,9},{9,10},{10,1... | collective-permute-start | bytes 1179656 | tf_op jit(solution)/shard_map/ppermute | solution.py:26
  97.2 7.9 %collective-permute-start.5 = (bf16[8,2,48,2048]{3,2,1,0:T(8,128)(2,1)}, bf16[8,2,48,2048]{3,2,1,0:T(8,128)(2,1)}, u32[]{:S(2)}, u32[]{:S(2)}) collective-permute-start(bf16[8,2,48,2048]{3,2,1,0:T(8,128)(2,1)} %shard_map.56), channel_id=1, source_target_pairs={{0,16},{16,0},{1,17},{17,1},{2,18},{18,2},{3,19},{19,3},{4,20},{20... | collective-permute-start | bytes 9437192 | tf_op jit(solution)/shard_map/ppermute | solution.py:26
  129.6 1.6 %copy-start = (bf16[32,24,2048]{2,1,0:T(8,128)(2,1)}, bf16[32,24,2048]{2,1,0:T(8,128)(2,1)S(1)}, u32[]{:S(2)}) copy-start(bf16[32,24,2048]{2,1,0:T(8,128)(2,1)S(1)} %all-to-all-done.1) | copy-start | bytes 9437188

commit v3 on v2

v3 whole, which is shorter than its diff:
```python
import math

import jax
import jax.numpy as jnp
from jax import lax
from jax.experimental import pallas as pl
from jax.experimental.pallas import tpu as pltpu
from jax.sharding import Mesh, PartitionSpec as P

STORE = ("z", "y_lo", "core")
PROD = ("y_two", "y_one", "x")
VMEM = pl.BlockSpec(memory_space=pltpu.VMEM)


def exchange(block, axis):
    return lax.all_to_all(block, axis, split_axis=0, concat_axis=0, tiled=True)


def gather(block, axis):
    count = lax.axis_size(axis)
    return exchange(jnp.broadcast_to(block[None], (count,) + block.shape), axis)


def shift(block, axis, by):
    count = lax.axis_size(axis)
    return lax.ppermute(block, axis, [(i, (i + by) % count) for i in range(count)])


def slots_of(targets, bucket):
    rows = targets.shape[1]
    above = lax.broadcasted_iota(jnp.int32, (rows, rows), 0)
    along = lax.broadcasted_iota(jnp.int32, (rows, rows), 1)
    upright = jnp.sum(jnp.where(above == along, targets, 0), axis=1, keepdims=True)
    earlier = jnp.where((upright == targets) & (above < along), 1, 0)
    return targets * bucket + jnp.sum(earlier, axis=0, keepdims=True)


def prepare(gradients, targets, left, right, bucket, capacity, step=1024):
    rows, width = gradients.shape
    deep, fine = left.shape[1], right.shape[0]
    steps = width // step

    def kernel(targets_ref, rows_ref, left_ref, right_ref, out_ref, product, squares, pick):
        i = pl.program_id(0)

        @pl.when(i == 0)
        def _():
            tiled = jnp.concatenate([right_ref[...]] * (step // fine), axis=1)
            above = lax.broadcasted_iota(jnp.int32, (deep, step), 0)
            along = lax.broadcasted_iota(jnp.int32, (deep, step), 1)
            total = jnp.zeros((rows, 1), jnp.float32)
            for j in range(steps):
                spread = lax.dot_general(
                    left_ref[...],
                    jnp.where(above == j * (step // fine) + along // fine, 1.0, 0.0),
                    (((0,), (0,)), ((), ())),
                    preferred_element_type=jnp.float32,
                    precision=lax.Precision.HIGHEST,
                )
                factor = (spread[:, None, :] * tiled[None]).reshape((width, step))
                high = factor.astype(jnp.bfloat16)
                low = (factor - high.astype(jnp.float32)).astype(jnp.bfloat16)
                part = jnp.dot(rows_ref[...], high, preferred_element_type=jnp.float32)
                part = part + jnp.dot(rows_ref[...], low, preferred_element_type=jnp.float32)
                product[j] = part
                total = total + jnp.sum(part * part, axis=1, keepdims=True)
            squares[...] = lax.rsqrt(total / width + 1e-06) * (1.0 / math.sqrt(width))
            slots = slots_of(targets_ref[...], bucket)
            at = lax.broadcasted_iota(jnp.int32, (capacity, rows), 0)
            pick[...] = jnp.where(at == slots, 1.0, 0.0).astype(jnp.bfloat16)

        @pl.when(i > 0)
        def _():
            normal = (product[i - 1] * squares[...]).astype(jnp.bfloat16)
            out_ref[...] = jnp.dot(
                pick[...], normal, preferred_element_type=jnp.float32
            ).astype(jnp.bfloat16)

    return pl.pallas_call(
        kernel,
        grid=(steps + 1,),
        in_specs=[
            pl.BlockSpec((1, rows), lambda i: (0, 0)),
            pl.BlockSpec((rows, width), lambda i: (0, 0)),
            pl.BlockSpec((deep, deep), lambda i: (0, 0)),
            pl.BlockSpec((fine, fine), lambda i: (0, 0)),
        ],
        out_specs=pl.BlockSpec((capacity, step), lambda i: (0, jnp.maximum(i - 1, 0))),
        out_shape=jax.ShapeDtypeStruct((capacity, width), jnp.bfloat16),
        scratch_shapes=[
            pltpu.VMEM((steps, rows, step), jnp.float32),
            pltpu.VMEM((rows, 1), jnp.float32),
            pltpu.VMEM((capacity, rows), jnp.bfloat16),
        ],
        compiler_params=pltpu.CompilerParams(vmem_limit_bytes=60 * 2**20),
        cost_estimate=pl.CostEstimate(
            flops=2 * rows * width * (2 * width + capacity),
            bytes_accessed=6 * 2**20,
            transcendentals=0,
        ),
    )(targets, gradients, left, right)


def reorder(place_of, pair, before, after, far, order):
    deep, high, own = order
    flips, rows, width = pair.shape
    outer = lax.axis_size("x")
    inner = high * outer * own
    total = outer * rows

    def kernel(at_ref, pair_ref, before_ref, after_ref, far0_ref, far1_ref, out_ref, held, sems):
        copies = []
        for flip, far_ref in enumerate((far0_ref, far1_ref)):
            sources = [ref.at[flip] for ref in (pair_ref, before_ref, after_ref)] + [far_ref]
            for s, source_ref in enumerate(sources):
                there = held.at[flip, pl.ds(s * rows, rows)]
                copies.append(pltpu.make_async_copy(source_ref, there, sems.at[flip, s]))
        for copy in copies:
            copy.start()
        to = lax.broadcasted_iota(jnp.int32, (total, total), 0)
        source = lax.broadcasted_iota(jnp.int32, (total, total), 1)
        slot = source // rows
        move = jnp.where(slot == 1, outer - 1, jnp.where(slot == 2, 1, jnp.where(slot == 3, 2, 0)))
        at_x = (at_ref[0] + move) % outer
        at_z = source % rows // (high * own)
        at_high = (source % (high * own) // own) ^ at_ref[3]
        goes = at_z * inner + (at_high * outer + at_x) * own + source % own
        pick = jnp.where(to == goes, 1.0, 0.0).astype(jnp.bfloat16)
        for copy in copies:
            copy.wait()
        for flip in range(flips):
            moved = jnp.dot(pick, held[flip], preferred_element_type=jnp.float32)
            where = (at_ref[1] + flip) % flips
            out_ref[:, pl.ds(where, 1)] = moved.astype(jnp.bfloat16).reshape((deep, 1, inner, width))

    hbm = pl.BlockSpec(memory_space=pltpu.HBM)
    return pl.pallas_call(
        kernel,
        in_specs=[pl.BlockSpec(memory_space=pltpu.SMEM)] + [hbm] * 5,
        out_specs=VMEM,
        out_shape=jax.ShapeDtypeStruct((deep, flips, inner, width), jnp.bfloat16),
        scratch_shapes=[
            pltpu.VMEM((flips, total, width), jnp.bfloat16),
            pltpu.SemaphoreType.DMA((flips, outer)),
        ],
        compiler_params=pltpu.CompilerParams(vmem_limit_bytes=60 * 2**20),
        cost_estimate=pl.CostEstimate(
            flops=6 * flips * total * total * width,
            bytes_accessed=4 * flips * total * width,
            transcendentals=0,
        ),
    )(place_of, pair, before, after, *far)


def score(place_of, own_core, other_core, stored):
    deep, flips, inner, width = own_core.shape
    capacity = stored.shape[0]
    blocks = deep * flips
    half = blocks // 2

    def kernel(at_ref, own_ref, other_ref, stored_ref, out_ref, held, sems):
        i = pl.program_id(0)
        copies = [
            pltpu.make_async_copy(
                (own_ref, other_ref)[j // 2].at[pl.ds(j % 2 * half, half)], held.at[j], sems.at[j]
            )
            for j in range(4)
        ]

        @pl.when(i == 0)
        def _():
            for copy in copies:
                copy.start()

        for j in range(4):

            @pl.when(i == j)
            def _():
                copies[j].wait()
                scores = lax.dot_general(
                    held[j].reshape((half * inner, width)),
                    stored_ref[...],
                    (((1,), (1,)), ((), ())),
                    preferred_element_type=jnp.float32,
                )
                out_ref[...] = scores.astype(jnp.bfloat16).reshape((half, 1, inner, capacity))

    hbm = pl.BlockSpec(memory_space=pltpu.HBM)
    own_core, other_core = (
        pltpu.with_memory_space_constraint(a.reshape((blocks, inner, width)), pltpu.HBM)
        for a in (own_core, other_core)
    )
    out = pl.pallas_call(
        kernel,
        grid_spec=pltpu.PrefetchScalarGridSpec(
            num_scalar_prefetch=1,
            grid=(4,),
            in_specs=[hbm, hbm, VMEM],
            out_specs=pl.BlockSpec(
                (half, 1, inner, capacity), lambda i, at: (i % 2, (at[2] + i // 2) % 2, 0, 0)
            ),
            scratch_shapes=[
                pltpu.VMEM((4, half, inner, width), jnp.bfloat16),
                pltpu.SemaphoreType.DMA((4,)),
            ],
        ),
        out_shape=jax.ShapeDtypeStruct((blocks, 2, inner, capacity), jnp.bfloat16),
        compiler_params=pltpu.CompilerParams(vmem_limit_bytes=24 * 2**20),
        cost_estimate=pl.CostEstimate(
            flops=4 * blocks * inner * capacity * width,
            bytes_accessed=12 * 2**20,
            transcendentals=0,
        ),
    )(place_of, own_core, other_core, stored)
    return out.reshape((-1, capacity))


def body(gradients, destinations, queries, left_factor, right_factor):
    owners = lax.axis_size(STORE)
    rows, width = gradients.shape
    bucket = 2 * rows // owners
    capacity = owners * bucket
    own = queries.shape[0]
    order = (lax.axis_size("z"), lax.axis_size(("y_two", "y_one")), own)

    line = queries.reshape((-1, 128))
    line = gather(jnp.stack([line, shift(line, "y_one", 1)]), ("z", "y_two"))
    buffer = prepare(gradients, destinations[None], left_factor, right_factor, bucket, capacity)
    line, buffer = lax.optimization_barrier((line, buffer))
    near = shift(line, "y_lo", 1)
    stored = exchange(buffer.reshape((owners, bucket, width)), STORE).reshape((capacity, width))

    pair = jnp.stack([line, near]).reshape((2, -1, width))
    before, after = shift(pair, "x", 1), shift(pair, "x", -1)
    far = (shift(before[0], "x", 1), shift(after[1], "x", -1))
    place_of = jnp.stack([lax.axis_index(a) for a in ("x", "y_lo", "core", "y_one")])
    place_of = place_of.astype(jnp.int32)
    mine = reorder(place_of, pair, before, after, far, order)
    others = shift(mine, "core", 1)
    return score(place_of, mine, others, stored)


def solution(mesh):
    fine = Mesh(mesh.devices.reshape((8, 2, 2, 2, 2, 4)), STORE + PROD)
    whole = STORE + PROD
    return jax.shard_map(
        body,
        mesh=fine,
        in_specs=(P(whole, None), P(whole), P(whole, None), P(), P()),
        out_specs=P(None, whole),
        check_vma=False,
    )
```

time: 144 us -> 141 us (0.979)
  local copies, waits for them, and re-layouts: 14.2 us -> 9.86 us
  Pallas kernels: 31.7 us -> 27.4 us
  starting transfers between devices: 42.9 us -> 45.7 us
  waiting for transfers between devices: 53.6 us -> 56.4 us
    ppermute x6 -> x7, starting transfers between devices: 18.8 us -> 25.4 us  [shift(): lax.ppermute(block, axis, [(i, (i + by) % count) for i in range(count)])]
    all_to_all x2, starting transfers between devices: 24.1 us -> 20.3 us  [exchange(): return lax.all_to_all(block, axis, split_axis=0, concat_axis=0, tiled=True)]
    pallas_call x1, Pallas kernels: 12 us -> 8.74 us  [score(): pl.pallas_call(kernel, grid_spec=pltpu.PrefetchScalarGridSpec(num_scalar_...]
    all_to_all x2, waiting for transfers between devices: 24.5 us -> 27.3 us  [exchange(): return lax.all_to_all(block, axis, split_axis=0, concat_axis=0, tiled=True)]
    unnamed x7, local copies, waits for them, and re-layouts: 4.29 us -> 2.66 us
    ppermute x6 -> x7, waiting for transfers between devices: 29.2 us -> 29.1 us  [shift(): lax.ppermute(block, axis, [(i, (i + by) % count) for i in range(count)])]
  transfers between devices with their start and end apart: 8 -> 9, of which waited for: 5 -> 8; matrix products, arithmetic and copies ran while one was open for 7% -> 6% of each run, Pallas kernels for 14% -> 13%
where the time goes in v3:
time: 141 us; the launch traced here: 140 us
  waiting for transfers between devices  56.4 us (40%)
  starting transfers between devices  45.7 us (32%)
  Pallas kernels  27.4 us (19%)
  local copies, waits for them, and re-layouts  9.86 us (7%)
    ppermute x7, waiting for transfers between devices, shift(): lax.ppermute(block, axis, [(i, (i + by) % count) for i in range(count)])  29.1 us
    all_to_all x2, waiting for transfers between devices, exchange(): return lax.all_to_all(block, axis, split_axis=0, concat_axis=0, tiled=True)  27.3 us
    ppermute x7, starting transfers between devices, shift(): lax.ppermute(block, axis, [(i, (i + by) % count) for i in range(count)])  25.4 us
    all_to_all x2, starting transfers between devices, exchange(): return lax.all_to_all(block, axis, split_axis=0, concat_axis=0, tiled=True)  20.3 us
    pallas_call x1, Pallas kernels, prepare(): pl.pallas_call(kernel, grid=(steps + 1,), in_specs=[pl.BlockSpec((1, rows...  12.7 us
    pallas_call x1, Pallas kernels, score(): pl.pallas_call(kernel, grid_spec=pltpu.PrefetchScalarGridSpec(num_scalar_...  8.74 us
    pallas_call x1, Pallas kernels, reorder(): pl.pallas_call(kernel, in_specs=[pl.BlockSpec(memory_space=pltpu.SMEM)] +...  6.02 us
    another operation x3, local copies, waits for them, and re-layouts, body(): pair = jnp.stack([line, near]).reshape((2, -1, width))  2.87 us
  transfers between devices with their start and end apart: 9, of which 8 were waited for; matrix products, arithmetic and copies ran while one was open for 6% of the time, Pallas kernels for 13%

profile of v3, /device:TPU:6, one launch (start us, length us, event | category | flops | bytes accessed | tf_op | source)
XLA Modules:
  0.0 140.3 jit_solution(14569646921887565771)
XLA Ops:
  0.7 4.5 %collective-permute-start = (bf16[48,128]{1,0:T(8,128)(2,1)S(1)}, bf16[48,128]{1,0:T(8,128)(2,1)S(1)}, u32[]{:S(2)}, u32[]{:S(2)}) collective-permute-start(bf16[48,128]{1,0:T(8,128)(2,1)S(1)} %reshape.24), channel_id=1, source_target_pairs={{0,4},{4,0},{1,5},{5,1},{2,6},{6,2},{3,7},{7,3},{8,12},{12,8},{9,1... | collective-permute-start | bytes 36872 | tf_op jit(solution)/shard_map/ppermute | solution.py:26
  6.0 1.2 collective-permute-done
  8.0 15.7 %all-to-all-start = ((bf16[16,2,48,128]{3,2,1,0:T(8,128)(2,1)}), bf16[16,2,48,128]{3,2,1,0:T(8,128)(2,1)S(1)}, u32[]{:S(2)}, u32[]{:S(2)}) async-start(bf16[16,2,48,128]{3,2,1,0:T(8,128)(2,1)} %broadcast_in_dim.4), calls=%async_computation | async-start | bytes 786432 | tf_op jit(solution)/shard_map/all_to_all | solution.py:16
  23.7 1.2 broadcast_in_dim.10.targets_ref
  25.0 12.7 %shard_map.55 = bf16[768,2048]{1,0:T(8,128)(2,1)} custom-call(s32[1,384]{1,0:T(1,128)} %broadcast_in_dim.10.targets_ref, bf16[384,2048]{1,0:T(8,128)(2,1)} %rows_ref.1, f32[32,32]{1,0:T(8,128)} %left_ref.1, f32[64,64]{1,0:T(8,128)} %right_ref.1), custom_call_target="tpu_custom_call" | custom-call | flops 7650410496 | bytes 6291456 | tf_op jit(solution)/shard_map/pallas_call | solution.py:79
  37.6 1.5 %all-to-all-done = bf16[16,2,48,128]{3,2,1,0:T(8,128)(2,1)S(1)} async-done(((bf16[16,2,48,128]{3,2,1,0:T(8,128)(2,1)}), bf16[16,2,48,128]{3,2,1,0:T(8,128)(2,1)S(1)}, u32[]{:S(2)}, u32[]{:S(2)}) %all-to-all-start) | async-done | bytes 393248 | tf_op jit(solution)/shard_map/all_to_all | solution.py:16
  39.2 4.7 %collective-permute-start.1 = (bf16[16,2,48,128]{3,2,1,0:T(8,128)(2,1)S(1)}, bf16[16,2,48,128]{3,2,1,0:T(8,128)(2,1)}, u32[]{:S(2)}, u32[]{:S(2)}) collective-permute-start(bf16[16,2,48,128]{3,2,1,0:T(8,128)(2,1)S(1)} %all-to-all-done), channel_id=1, source_target_pairs={{0,32},{32,0},{1,33},{33,1},{2,34},{34,2},{3,35},{35,3},{4,36},{36... | collective-permute-start | bytes 1179656 | tf_op jit(solution)/shard_map/ppermute | solution.py:26
  43.9 4.6 %all-to-all-start.1 = ((bf16[32,24,2048]{2,1,0:T(8,128)(2,1)}), bf16[32,24,2048]{2,1,0:T(8,128)(2,1)S(1)}, u32[]{:S(2)}, u32[]{:S(2)}) async-start(bf16[32,24,2048]{2,1,0:T(8,128)(2,1)} %bitcast.19), calls=%async_computation.1 | async-start | bytes 6291456 | tf_op jit(solution)/shard_map/all_to_all | solution.py:16
  48.5 0.9 stack.37
  49.5 1.8 %constant_dynamic-update-slice_fusion.1 = bf16[2,96,2048]{2,1,0:T(8,128)(2,1)} fusion(bf16[1,96,2048]{2,1,0:T(8,128)(2,1)} %stack.37), kind=kLoop, calls=%fused_computation.4 | loop fusion | bytes 786432
  51.2 1.2 collective-permute-done.1
  52.4 1.2 stack.38
  54.4 2.7 %collective-permute-start.3 = (bf16[2,96,2048]{2,1,0:T(8,128)(2,1)}, bf16[2,96,2048]{2,1,0:T(8,128)(2,1)S(1)}, u32[]{:S(2)}, u32[]{:S(2)}) collective-permute-start(bf16[2,96,2048]{2,1,0:T(8,128)(2,1)} %constant_dynamic-update-slice_fusion.pair_ref), channel_id=1, source_target_pairs={{0,3},{1,0},{2,1},{3,2},{4,7},{5,4},{6,5},{7,6},{8,11},{9,8},{10,9... | collective-permute-start | bytes 2359304 | tf_op jit(solution)/shard_map/ppermute | solution.py:26
  57.1 4.3 %collective-permute-start.2 = (bf16[2,96,2048]{2,1,0:T(8,128)(2,1)}, bf16[2,96,2048]{2,1,0:T(8,128)(2,1)S(1)}, u32[]{:S(2)}, u32[]{:S(2)}) collective-permute-start(bf16[2,96,2048]{2,1,0:T(8,128)(2,1)} %constant_dynamic-update-slice_fusion.pair_ref), channel_id=1, source_target_pairs={{0,1},{1,2},{2,3},{3,0},{4,5},{5,6},{6,7},{7,4},{8,9},{9,10},{10,1... | collective-permute-start | bytes 2359304 | tf_op jit(solution)/shard_map/ppermute | solution.py:26
  61.4 14.8 %collective-permute-done.3.after_ref = bf16[2,96,2048]{2,1,0:T(8,128)(2,1)S(1)} collective-permute-done((bf16[2,96,2048]{2,1,0:T(8,128)(2,1)}, bf16[2,96,2048]{2,1,0:T(8,128)(2,1)S(1)}, u32[]{:S(2)}, u32[]{:S(2)}) %collective-permute-start.3) | collective-permute-done | bytes 786464 | tf_op jit(solution)/shard_map/ppermute | solution.py:26
  76.2 1.9 %collective-permute-start.5 = (bf16[96,2048]{1,0:T(8,128)(2,1)S(1)}, bf16[96,2048]{1,0:T(8,128)(2,1)}, u32[]{:S(2)}, u32[]{:S(2)}) collective-permute-start(bf16[96,2048]{1,0:T(8,128)(2,1)S(1)} %slice_bitcast_fusion), channel_id=1, source_target_pairs={{0,3},{1,0},{2,1},{3,2},{4,7},{5,4},{6,5},{7,6},{8,11},{9,8},{10,9... | collective-permute-start | bytes 1179656 | tf_op jit(solution)/shard_map/ppermute | solution.py:26
  79.9 5.1 %collective-permute-start.4 = (bf16[96,2048]{1,0:T(8,128)(2,1)}, bf16[96,2048]{1,0:T(8,128)(2,1)}, u32[]{:S(2)}, u32[]{:S(2)}) collective-permute-start(bf16[96,2048]{1,0:T(8,128)(2,1)} %slice_bitcast_fusion.1), channel_id=1, source_target_pairs={{0,1},{1,2},{2,3},{3,0},{4,5},{5,6},{6,7},{7,4},{8,9},{9,10},{10,1... | collective-permute-start | bytes 1179656 | tf_op jit(solution)/shard_map/ppermute | solution.py:26
  85.7 3.0 %collective-permute-done.5.far1_ref = bf16[96,2048]{1,0:T(8,128)(2,1)} collective-permute-done((bf16[96,2048]{1,0:T(8,128)(2,1)S(1)}, bf16[96,2048]{1,0:T(8,128)(2,1)}, u32[]{:S(2)}, u32[]{:S(2)}) %collective-permute-start.5) | collective-permute-done | bytes 393248 | tf_op jit(solution)/shard_map/ppermute | solution.py:26
  88.6 3.1 %collective-permute-done.4.far0_ref = bf16[96,2048]{1,0:T(8,128)(2,1)} collective-permute-done((bf16[96,2048]{1,0:T(8,128)(2,1)}, bf16[96,2048]{1,0:T(8,128)(2,1)}, u32[]{:S(2)}, u32[]{:S(2)}) %collective-permute-start.4) | collective-permute-done | bytes 393248 | tf_op jit(solution)/shard_map/ppermute | solution.py:26
  91.7 6.0 %shard_map.56 = bf16[8,2,48,2048]{3,2,1,0:T(8,128)(2,1)} custom-call(s32[4]{0:T(128)} %pad_add_fusion.at_ref, bf16[2,96,2048]{2,1,0:T(8,128)(2,1)} %constant_dynamic-update-slice_fusion.pair_ref, bf16[2,96,2048]{2,1,0:T(8,128)(2,1)} %copy-done.2, bf16[2,96,2048]{2,1,0:T(8,128)(2,1)} %copy-done.1, bf16[96,2048]{1,0:T(8,128)(2,1)} %collective-permute-done.4.far0_ref, ...), custom_call_target="tpu_custom_call" | custom-call | flops 3623878656 | bytes 6291456 | tf_op jit(solution)/shard_map/pallas_call | solution.py:137
  97.8 2.1 %collective-permute-start.6 = (bf16[8,2,48,2048]{3,2,1,0:T(8,128)(2,1)}, bf16[8,2,48,2048]{3,2,1,0:T(8,128)(2,1)}, u32[]{:S(2)}, u32[]{:S(2)}) collective-permute-start(bf16[8,2,48,2048]{3,2,1,0:T(8,128)(2,1)} %shard_map.56), channel_id=1, source_target_pairs={{0,16},{16,0},{1,17},{17,1},{2,18},{18,2},{3,19},{19,3},{4,20},{20... | collective-permute-start | bytes 9437192 | tf_op jit(solution)/shard_map/ppermute | solution.py:26
  99.9 5.8 %collective-permute-done.6 = bf16[8,2,48,2048]{3,2,1,0:T(8,128)(2,1)} collective-permute-done((bf16[8,2,48,2048]{3,2,1,0:T(8,128)(2,1)}, bf16[8,2,48,2048]{3,2,1,0:T(8,128)(2,1)}, u32[]{:S(2)}, u32[]{:S(2)}) %collective-permute-start.6) | collective-permute-done | bytes 3145760 | tf_op jit(solution)/shard_map/ppermute | solution.py:26
  105.7 25.8 %all-to-all-done.1 = bf16[32,24,2048]{2,1,0:T(8,128)(2,1)S(1)} async-done(((bf16[32,24,2048]{2,1,0:T(8,128)(2,1)}), bf16[32,24,2048]{2,1,0:T(8,128)(2,1)S(1)}, u32[]{:S(2)}, u32[]{:S(2)}) %all-to-all-start.1) | async-done | bytes 3145760 | tf_op jit(solution)/shard_map/all_to_all | solution.py:16
  131.4 8.7 %shard_map.57 = bf16[16,2,48,768]{3,2,1,0:T(8,128)(2,1)} custom-call(s32[4]{0:T(128)S(1)} %copy-done, bf16[16,48,2048]{2,1,0:T(8,128)(2,1)} %bitcast.21, bf16[16,48,2048]{2,1,0:T(8,128)(2,1)} %bitcast.8.other_ref, bf16[768,2048]{1,0:T(8,128)(2,1)S(1)} %bitcast.18), custom_call_target="tpu_custom_call" | custom-call | flops 4831838208 | bytes 12582912 | tf_op jit(solution)/shard_map/pallas_call | solution.py:193
  (15 shorter events, 5.4 us)
Async XLA Ops:
  0.7 6.5 %collective-permute-start = (bf16[48,128]{1,0:T(8,128)(2,1)S(1)}, bf16[48,128]{1,0:T(8,128)(2,1)S(1)}, u32[]{:S(2)}, u32[]{:S(2)}) collective-permute-start(bf16[48,128]{1,0:T(8,128)(2,1)S(1)} %reshape.24), channel_id=1, source_target_pairs={{0,4},{4,0},{1,5},{5,1},{2,6},{6,2},{3,7},{7,3},{8,12},{12,8},{9,1... | collective-permute-start | bytes 36872 | tf_op jit(solution)/shard_map/ppermute | solution.py:26
  8.0 31.1 %all-to-all-start = ((bf16[16,2,48,128]{3,2,1,0:T(8,128)(2,1)}), bf16[16,2,48,128]{3,2,1,0:T(8,128)(2,1)S(1)}, u32[]{:S(2)}, u32[]{:S(2)}) async-start(bf16[16,2,48,128]{3,2,1,0:T(8,128)(2,1)} %broadcast_in_dim.4), calls=%async_computation | async-start | bytes 786432 | tf_op jit(solution)/shard_map/all_to_all | solution.py:16
  39.2 13.2 %collective-permute-start.1 = (bf16[16,2,48,128]{3,2,1,0:T(8,128)(2,1)S(1)}, bf16[16,2,48,128]{3,2,1,0:T(8,128)(2,1)}, u32[]{:S(2)}, u32[]{:S(2)}) collective-permute-start(bf16[16,2,48,128]{3,2,1,0:T(8,128)(2,1)S(1)} %all-to-all-done), channel_id=1, source_target_pairs={{0,32},{32,0},{1,33},{33,1},{2,34},{34,2},{3,35},{35,3},{4,36},{36... | collective-permute-start | bytes 1179656 | tf_op jit(solution)/shard_map/ppermute | solution.py:26
  43.9 87.5 %all-to-all-start.1 = ((bf16[32,24,2048]{2,1,0:T(8,128)(2,1)}), bf16[32,24,2048]{2,1,0:T(8,128)(2,1)S(1)}, u32[]{:S(2)}, u32[]{:S(2)}) async-start(bf16[32,24,2048]{2,1,0:T(8,128)(2,1)} %bitcast.19), calls=%async_computation.1 | async-start | bytes 6291456 | tf_op jit(solution)/shard_map/all_to_all | solution.py:16
  54.4 21.8 %collective-permute-start.3 = (bf16[2,96,2048]{2,1,0:T(8,128)(2,1)}, bf16[2,96,2048]{2,1,0:T(8,128)(2,1)S(1)}, u32[]{:S(2)}, u32[]{:S(2)}) collective-permute-start(bf16[2,96,2048]{2,1,0:T(8,128)(2,1)} %constant_dynamic-update-slice_fusion.pair_ref), channel_id=1, source_target_pairs={{0,3},{1,0},{2,1},{3,2},{4,7},{5,4},{6,5},{7,6},{8,11},{9,8},{10,9... | collective-permute-start | bytes 2359304 | tf_op jit(solution)/shard_map/ppermute | solution.py:26
  57.1 21.1 %collective-permute-start.2 = (bf16[2,96,2048]{2,1,0:T(8,128)(2,1)}, bf16[2,96,2048]{2,1,0:T(8,128)(2,1)S(1)}, u32[]{:S(2)}, u32[]{:S(2)}) collective-permute-start(bf16[2,96,2048]{2,1,0:T(8,128)(2,1)} %constant_dynamic-update-slice_fusion.pair_ref), channel_id=1, source_target_pairs={{0,1},{1,2},{2,3},{3,0},{4,5},{5,6},{6,7},{7,4},{8,9},{9,10},{10,1... | collective-permute-start | bytes 2359304 | tf_op jit(solution)/shard_map/ppermute | solution.py:26
  76.2 2.0 %copy-start.1 = (bf16[2,96,2048]{2,1,0:T(8,128)(2,1)}, bf16[2,96,2048]{2,1,0:T(8,128)(2,1)S(1)}, u32[]{:S(2)}) copy-start(bf16[2,96,2048]{2,1,0:T(8,128)(2,1)S(1)} %collective-permute-done.3.after_ref) | copy-start | bytes 2359300
  76.2 12.4 %collective-permute-start.5 = (bf16[96,2048]{1,0:T(8,128)(2,1)S(1)}, bf16[96,2048]{1,0:T(8,128)(2,1)}, u32[]{:S(2)}, u32[]{:S(2)}) collective-permute-start(bf16[96,2048]{1,0:T(8,128)(2,1)S(1)} %slice_bitcast_fusion), channel_id=1, source_target_pairs={{0,3},{1,0},{2,1},{3,2},{4,7},{5,4},{6,5},{7,6},{8,11},{9,8},{10,9... | collective-permute-start | bytes 1179656 | tf_op jit(solution)/shard_map/ppermute | solution.py:26
  78.2 0.9 copy-start.2
  79.9 11.9 %collective-permute-start.4 = (bf16[96,2048]{1,0:T(8,128)(2,1)}, bf16[96,2048]{1,0:T(8,128)(2,1)}, u32[]{:S(2)}, u32[]{:S(2)}) collective-permute-start(bf16[96,2048]{1,0:T(8,128)(2,1)} %slice_bitcast_fusion.1), channel_id=1, source_target_pairs={{0,1},{1,2},{2,3},{3,0},{4,5},{5,6},{6,7},{7,4},{8,9},{9,10},{10,1... | collective-permute-start | bytes 1179656 | tf_op jit(solution)/shard_map/ppermute | solution.py:26
  85.6 45.8 %copy-start = (s32[4]{0:T(128)S(1)}, s32[4]{0:T(128)}, u32[]{:S(2)}) copy-start(s32[4]{0:T(128)} %pad_add_fusion.at_ref) | copy-start | bytes 52
  97.8 7.9 %collective-permute-start.6 = (bf16[8,2,48,2048]{3,2,1,0:T(8,128)(2,1)}, bf16[8,2,48,2048]{3,2,1,0:T(8,128)(2,1)}, u32[]{:S(2)}, u32[]{:S(2)}) collective-permute-start(bf16[8,2,48,2048]{3,2,1,0:T(8,128)(2,1)} %shard_map.56), channel_id=1, source_target_pairs={{0,16},{16,0},{1,17},{17,1},{2,18},{18,2},{3,19},{19,3},{4,20},{20... | collective-permute-start | bytes 9437192 | tf_op jit(solution)/shard_map/ppermute | solution.py:26

commit v4 on v3

--- a/solution.py
+++ b/solution.py
@@ -8,7 +8,7 @@
 from jax.sharding import Mesh, PartitionSpec as P
 
 STORE = ("z", "y_lo", "core")
-PROD = ("y_two", "y_one", "x")
+PROD = ("y_hi", "x")
 VMEM = pl.BlockSpec(memory_space=pltpu.VMEM)
 
 
@@ -123,7 +123,7 @@
         move = jnp.where(slot == 1, outer - 1, jnp.where(slot == 2, 1, jnp.where(slot == 3, 2, 0)))
         at_x = (at_ref[0] + move) % outer
         at_z = source % rows // (high * own)
-        at_high = (source % (high * own) // own) ^ at_ref[3]
+        at_high = source % (high * own) // own
         goes = at_z * inner + (at_high * outer + at_x) * own + source % own
         pick = jnp.where(to == goes, 1.0, 0.0).astype(jnp.bfloat16)
         for copy in copies:
@@ -221,10 +221,9 @@
     bucket = 2 * rows // owners
     capacity = owners * bucket
     own = queries.shape[0]
-    order = (lax.axis_size("z"), lax.axis_size(("y_two", "y_one")), own)
-
-    line = queries.reshape((-1, 128))
-    line = gather(jnp.stack([line, shift(line, "y_one", 1)]), ("z", "y_two"))
+    order = (lax.axis_size("z"), lax.axis_size("y_hi"), own)
+
+    line = gather(queries.reshape((-1, 128)), ("z", "y_hi"))
     buffer = prepare(gradients, destinations[None], left_factor, right_factor, bucket, capacity)
     line, buffer = lax.optimization_barrier((line, buffer))
     near = shift(line, "y_lo", 1)
@@ -233,15 +232,14 @@
     pair = jnp.stack([line, near]).reshape((2, -1, width))
     before, after = shift(pair, "x", 1), shift(pair, "x", -1)
     far = (shift(before[0], "x", 1), shift(after[1], "x", -1))
-    place_of = jnp.stack([lax.axis_index(a) for a in ("x", "y_lo", "core", "y_one")])
-    place_of = place_of.astype(jnp.int32)
+    place_of = jnp.stack([lax.axis_index(a) for a in ("x", "y_lo", "core")]).astype(jnp.int32)
     mine = reorder(place_of, pair, before, after, far, order)
     others = shift(mine, "core", 1)
     return score(place_of, mine, others, stored)
 
 
 def solution(mesh):
-    fine = Mesh(mesh.devices.reshape((8, 2, 2, 2, 2, 4)), STORE + PROD)
+    fine = Mesh(mesh.devices.reshape((8, 2, 2, 4, 4)), STORE + PROD)
     whole = STORE + PROD
     return jax.shard_map(
         body,

time: 141 us -> 135 us (0.957)
  starting transfers between devices: 45.7 us -> 40.2 us
    ppermute x7 -> x6, starting transfers between devices: 25.4 us -> 18.1 us  [shift(): lax.ppermute(block, axis, [(i, (i + by) % count) for i in range(count)])]
    all_to_all x2, starting transfers between devices: 20.3 us -> 22.1 us  [exchange(): return lax.all_to_all(block, axis, split_axis=0, concat_axis=0, tiled=True)]
    ppermute x7 -> x6, waiting for transfers between devices: 29.1 us -> 28.9 us  [shift(): lax.ppermute(block, axis, [(i, (i + by) % count) for i in range(count)])]
  transfers between devices with their start and end apart: 9 -> 8, of which waited for: 8 -> 7; matrix products, arithmetic and copies ran while one was open for 6% -> 5% of each run, Pallas kernels for 13% -> 14%
where the time goes in v4:
time: 135 us; the launch traced here: 134 us
  waiting for transfers between devices  56.3 us (42%)
  starting transfers between devices  40.2 us (30%)
  Pallas kernels  27.4 us (20%)
  local copies, waits for them, and re-layouts  9.14 us (7%)
    ppermute x6, waiting for transfers between devices, shift(): lax.ppermute(block, axis, [(i, (i + by) % count) for i in range(count)])  28.9 us
    all_to_all x2, waiting for transfers between devices, exchange(): return lax.all_to_all(block, axis, split_axis=0, concat_axis=0, tiled=True)  27.4 us
    all_to_all x2, starting transfers between devices, exchange(): return lax.all_to_all(block, axis, split_axis=0, concat_axis=0, tiled=True)  22.1 us
    ppermute x6, starting transfers between devices, shift(): lax.ppermute(block, axis, [(i, (i + by) % count) for i in range(count)])  18.1 us
    pallas_call x1, Pallas kernels, prepare(): pl.pallas_call(kernel, grid=(steps + 1,), in_specs=[pl.BlockSpec((1, rows...  12.7 us
    pallas_call x1, Pallas kernels, score(): pl.pallas_call(kernel, grid_spec=pltpu.PrefetchScalarGridSpec(num_scalar_...  8.74 us
    pallas_call x1, Pallas kernels, reorder(): pl.pallas_call(kernel, in_specs=[pl.BlockSpec(memory_space=pltpu.SMEM)] +...  6.02 us
    another operation x3, local copies, waits for them, and re-layouts, body(): pair = jnp.stack([line, near]).reshape((2, -1, width))  2.88 us
  transfers between devices with their start and end apart: 8, of which 7 were waited for; matrix products, arithmetic and copies ran while one was open for 5% of the time, Pallas kernels for 14%

profile of v4, /device:TPU:6, one launch (start us, length us, event | category | flops | bytes accessed | tf_op | source)
XLA Modules:
  0.0 134.0 jit_solution(5281118296436012832)
XLA Ops:
  0.7 0.8 broadcast_in_dim.11
  1.5 16.0 %all-to-all-start = ((bf16[32,48,128]{2,1,0:T(8,128)(2,1)}), bf16[32,48,128]{2,1,0:T(8,128)(2,1)S(1)}, u32[]{:S(2)}, u32[]{:S(2)}) async-start(bf16[32,48,128]{2,1,0:T(8,128)(2,1)} %broadcast_in_dim.11), calls=%async_computation | async-start | bytes 786432 | tf_op jit(solution)/shard_map/all_to_all | solution.py:16
  17.5 1.3 broadcast_in_dim.12.targets_ref
  18.8 12.7 %shard_map.55 = bf16[768,2048]{1,0:T(8,128)(2,1)} custom-call(s32[1,384]{1,0:T(1,128)} %broadcast_in_dim.12.targets_ref, bf16[384,2048]{1,0:T(8,128)(2,1)} %rows_ref.1, f32[32,32]{1,0:T(8,128)} %left_ref.1, f32[64,64]{1,0:T(8,128)} %right_ref.1), custom_call_target="tpu_custom_call" | custom-call | flops 7650410496 | bytes 6291456 | tf_op jit(solution)/shard_map/pallas_call | solution.py:79
  31.5 2.7 %all-to-all-done = bf16[32,48,128]{2,1,0:T(8,128)(2,1)S(1)} async-done(((bf16[32,48,128]{2,1,0:T(8,128)(2,1)}), bf16[32,48,128]{2,1,0:T(8,128)(2,1)S(1)}, u32[]{:S(2)}, u32[]{:S(2)}) %all-to-all-start) | async-done | bytes 393248 | tf_op jit(solution)/shard_map/all_to_all | solution.py:16
  34.2 1.9 %collective-permute-start = (bf16[32,48,128]{2,1,0:T(8,128)(2,1)S(1)}, bf16[32,48,128]{2,1,0:T(8,128)(2,1)}, u32[]{:S(2)}, u32[]{:S(2)}) collective-permute-start(bf16[32,48,128]{2,1,0:T(8,128)(2,1)S(1)} %all-to-all-done), channel_id=1, source_target_pairs={{0,32},{32,0},{1,33},{33,1},{2,34},{34,2},{3,35},{35,3},{4,36},{36... | collective-permute-start | bytes 1179656 | tf_op jit(solution)/shard_map/ppermute | solution.py:26
  36.1 6.1 %all-to-all-start.1 = ((bf16[32,24,2048]{2,1,0:T(8,128)(2,1)}), bf16[32,24,2048]{2,1,0:T(8,128)(2,1)S(1)}, u32[]{:S(2)}, u32[]{:S(2)}) async-start(bf16[32,24,2048]{2,1,0:T(8,128)(2,1)} %bitcast.13), calls=%async_computation.1 | async-start | bytes 6291456 | tf_op jit(solution)/shard_map/all_to_all | solution.py:16
  42.2 0.9 stack.25
  43.2 1.8 %constant_dynamic-update-slice_fusion.1 = bf16[2,96,2048]{2,1,0:T(8,128)(2,1)} fusion(bf16[1,96,2048]{2,1,0:T(8,128)(2,1)} %stack.25), kind=kLoop, calls=%fused_computation.3 | loop fusion | bytes 786432
  45.2 1.2 stack.26
  46.3 0.8 constant_dynamic-update-slice_fusion.pair_ref
  47.1 2.7 %collective-permute-start.2 = (bf16[2,96,2048]{2,1,0:T(8,128)(2,1)}, bf16[2,96,2048]{2,1,0:T(8,128)(2,1)S(1)}, u32[]{:S(2)}, u32[]{:S(2)}) collective-permute-start(bf16[2,96,2048]{2,1,0:T(8,128)(2,1)} %constant_dynamic-update-slice_fusion.pair_ref), channel_id=1, source_target_pairs={{0,3},{1,0},{2,1},{3,2},{4,7},{5,4},{6,5},{7,6},{8,11},{9,8},{10,9... | collective-permute-start | bytes 2359304 | tf_op jit(solution)/shard_map/ppermute | solution.py:26
  49.8 4.3 %collective-permute-start.1 = (bf16[2,96,2048]{2,1,0:T(8,128)(2,1)}, bf16[2,96,2048]{2,1,0:T(8,128)(2,1)S(1)}, u32[]{:S(2)}, u32[]{:S(2)}) collective-permute-start(bf16[2,96,2048]{2,1,0:T(8,128)(2,1)} %constant_dynamic-update-slice_fusion.pair_ref), channel_id=1, source_target_pairs={{0,1},{1,2},{2,3},{3,0},{4,5},{5,6},{6,7},{7,4},{8,9},{9,10},{10,1... | collective-permute-start | bytes 2359304 | tf_op jit(solution)/shard_map/ppermute | solution.py:26
  54.2 15.7 %collective-permute-done.2.after_ref = bf16[2,96,2048]{2,1,0:T(8,128)(2,1)S(1)} collective-permute-done((bf16[2,96,2048]{2,1,0:T(8,128)(2,1)}, bf16[2,96,2048]{2,1,0:T(8,128)(2,1)S(1)}, u32[]{:S(2)}, u32[]{:S(2)}) %collective-permute-start.2) | collective-permute-done | bytes 786464 | tf_op jit(solution)/shard_map/ppermute | solution.py:26
  69.9 1.9 %collective-permute-start.4 = (bf16[96,2048]{1,0:T(8,128)(2,1)S(1)}, bf16[96,2048]{1,0:T(8,128)(2,1)}, u32[]{:S(2)}, u32[]{:S(2)}) collective-permute-start(bf16[96,2048]{1,0:T(8,128)(2,1)S(1)} %slice_bitcast_fusion), channel_id=1, source_target_pairs={{0,3},{1,0},{2,1},{3,2},{4,7},{5,4},{6,5},{7,6},{8,11},{9,8},{10,9... | collective-permute-start | bytes 1179656 | tf_op jit(solution)/shard_map/ppermute | solution.py:26
  71.9 0.9 copy-done.2
  73.6 5.1 %collective-permute-start.3 = (bf16[96,2048]{1,0:T(8,128)(2,1)}, bf16[96,2048]{1,0:T(8,128)(2,1)}, u32[]{:S(2)}, u32[]{:S(2)}) collective-permute-start(bf16[96,2048]{1,0:T(8,128)(2,1)} %slice_bitcast_fusion.1), channel_id=1, source_target_pairs={{0,1},{1,2},{2,3},{3,0},{4,5},{5,6},{6,7},{7,4},{8,9},{9,10},{10,1... | collective-permute-start | bytes 1179656 | tf_op jit(solution)/shard_map/ppermute | solution.py:26
  79.3 4.1 %collective-permute-done.4.far1_ref = bf16[96,2048]{1,0:T(8,128)(2,1)} collective-permute-done((bf16[96,2048]{1,0:T(8,128)(2,1)S(1)}, bf16[96,2048]{1,0:T(8,128)(2,1)}, u32[]{:S(2)}, u32[]{:S(2)}) %collective-permute-start.4) | collective-permute-done | bytes 393248 | tf_op jit(solution)/shard_map/ppermute | solution.py:26
  83.4 3.1 %collective-permute-done.3.far0_ref = bf16[96,2048]{1,0:T(8,128)(2,1)} collective-permute-done((bf16[96,2048]{1,0:T(8,128)(2,1)}, bf16[96,2048]{1,0:T(8,128)(2,1)}, u32[]{:S(2)}, u32[]{:S(2)}) %collective-permute-start.3) | collective-permute-done | bytes 393248 | tf_op jit(solution)/shard_map/ppermute | solution.py:26
  86.4 6.0 %shard_map.56 = bf16[8,2,48,2048]{3,2,1,0:T(8,128)(2,1)} custom-call(s32[3]{0:T(128)} %pad_add_fusion.at_ref, bf16[2,96,2048]{2,1,0:T(8,128)(2,1)} %constant_dynamic-update-slice_fusion.pair_ref, bf16[2,96,2048]{2,1,0:T(8,128)(2,1)} %copy-done.2, bf16[2,96,2048]{2,1,0:T(8,128)(2,1)} %copy-done.1, bf16[96,2048]{1,0:T(8,128)(2,1)} %collective-permute-done.3.far0_ref, ...), custom_call_target="tpu_custom_call" | custom-call | flops 3623878656 | bytes 6291456 | tf_op jit(solution)/shard_map/pallas_call | solution.py:137
  92.5 2.1 %collective-permute-start.5 = (bf16[8,2,48,2048]{3,2,1,0:T(8,128)(2,1)}, bf16[8,2,48,2048]{3,2,1,0:T(8,128)(2,1)}, u32[]{:S(2)}, u32[]{:S(2)}) collective-permute-start(bf16[8,2,48,2048]{3,2,1,0:T(8,128)(2,1)} %shard_map.56), channel_id=1, source_target_pairs={{0,16},{16,0},{1,17},{17,1},{2,18},{18,2},{3,19},{19,3},{4,20},{20... | collective-permute-start | bytes 9437192 | tf_op jit(solution)/shard_map/ppermute | solution.py:26
  94.6 5.8 %collective-permute-done.5 = bf16[8,2,48,2048]{3,2,1,0:T(8,128)(2,1)} collective-permute-done((bf16[8,2,48,2048]{3,2,1,0:T(8,128)(2,1)}, bf16[8,2,48,2048]{3,2,1,0:T(8,128)(2,1)}, u32[]{:S(2)}, u32[]{:S(2)}) %collective-permute-start.5) | collective-permute-done | bytes 3145760 | tf_op jit(solution)/shard_map/ppermute | solution.py:26
  100.4 24.7 %all-to-all-done.1 = bf16[32,24,2048]{2,1,0:T(8,128)(2,1)S(1)} async-done(((bf16[32,24,2048]{2,1,0:T(8,128)(2,1)}), bf16[32,24,2048]{2,1,0:T(8,128)(2,1)S(1)}, u32[]{:S(2)}, u32[]{:S(2)}) %all-to-all-start.1) | async-done | bytes 3145760 | tf_op jit(solution)/shard_map/all_to_all | solution.py:16
  125.1 8.7 %shard_map.57 = bf16[16,2,48,768]{3,2,1,0:T(8,128)(2,1)} custom-call(s32[3]{0:T(128)S(1)} %copy-done, bf16[16,48,2048]{2,1,0:T(8,128)(2,1)} %bitcast.14, bf16[16,48,2048]{2,1,0:T(8,128)(2,1)} %bitcast.6.other_ref, bf16[768,2048]{1,0:T(8,128)(2,1)S(1)} %bitcast.12), custom_call_target="tpu_custom_call" | custom-call | flops 4831838208 | bytes 12582912 | tf_op jit(solution)/shard_map/pallas_call | solution.py:193
  (11 shorter events, 2.4 us)
Async XLA Ops:
  1.5 32.6 %all-to-all-start = ((bf16[32,48,128]{2,1,0:T(8,128)(2,1)}), bf16[32,48,128]{2,1,0:T(8,128)(2,1)S(1)}, u32[]{:S(2)}, u32[]{:S(2)}) async-start(bf16[32,48,128]{2,1,0:T(8,128)(2,1)} %broadcast_in_dim.11), calls=%async_computation | async-start | bytes 786432 | tf_op jit(solution)/shard_map/all_to_all | solution.py:16
  34.2 11.0 %collective-permute-start = (bf16[32,48,128]{2,1,0:T(8,128)(2,1)S(1)}, bf16[32,48,128]{2,1,0:T(8,128)(2,1)}, u32[]{:S(2)}, u32[]{:S(2)}) collective-permute-start(bf16[32,48,128]{2,1,0:T(8,128)(2,1)S(1)} %all-to-all-done), channel_id=1, source_target_pairs={{0,32},{32,0},{1,33},{33,1},{2,34},{34,2},{3,35},{35,3},{4,36},{36... | collective-permute-start | bytes 1179656 | tf_op jit(solution)/shard_map/ppermute | solution.py:26
  36.1 89.0 %all-to-all-start.1 = ((bf16[32,24,2048]{2,1,0:T(8,128)(2,1)}), bf16[32,24,2048]{2,1,0:T(8,128)(2,1)S(1)}, u32[]{:S(2)}, u32[]{:S(2)}) async-start(bf16[32,24,2048]{2,1,0:T(8,128)(2,1)} %bitcast.13), calls=%async_computation.1 | async-start | bytes 6291456 | tf_op jit(solution)/shard_map/all_to_all | solution.py:16
  47.1 22.8 %collective-permute-start.2 = (bf16[2,96,2048]{2,1,0:T(8,128)(2,1)}, bf16[2,96,2048]{2,1,0:T(8,128)(2,1)S(1)}, u32[]{:S(2)}, u32[]{:S(2)}) collective-permute-start(bf16[2,96,2048]{2,1,0:T(8,128)(2,1)} %constant_dynamic-update-slice_fusion.pair_ref), channel_id=1, source_target_pairs={{0,3},{1,0},{2,1},{3,2},{4,7},{5,4},{6,5},{7,6},{8,11},{9,8},{10,9... | collective-permute-start | bytes 2359304 | tf_op jit(solution)/shard_map/ppermute | solution.py:26
  49.8 22.0 %collective-permute-start.1 = (bf16[2,96,2048]{2,1,0:T(8,128)(2,1)}, bf16[2,96,2048]{2,1,0:T(8,128)(2,1)S(1)}, u32[]{:S(2)}, u32[]{:S(2)}) collective-permute-start(bf16[2,96,2048]{2,1,0:T(8,128)(2,1)} %constant_dynamic-update-slice_fusion.pair_ref), channel_id=1, source_target_pairs={{0,1},{1,2},{2,3},{3,0},{4,5},{5,6},{6,7},{7,4},{8,9},{9,10},{10,1... | collective-permute-start | bytes 2359304 | tf_op jit(solution)/shard_map/ppermute | solution.py:26
  69.9 2.0 %copy-start.1 = (bf16[2,96,2048]{2,1,0:T(8,128)(2,1)}, bf16[2,96,2048]{2,1,0:T(8,128)(2,1)S(1)}, u32[]{:S(2)}) copy-start(bf16[2,96,2048]{2,1,0:T(8,128)(2,1)S(1)} %collective-permute-done.2.after_ref) | copy-start | bytes 2359300
  69.9 13.4 %collective-permute-start.4 = (bf16[96,2048]{1,0:T(8,128)(2,1)S(1)}, bf16[96,2048]{1,0:T(8,128)(2,1)}, u32[]{:S(2)}, u32[]{:S(2)}) collective-permute-start(bf16[96,2048]{1,0:T(8,128)(2,1)S(1)} %slice_bitcast_fusion), channel_id=1, source_target_pairs={{0,3},{1,0},{2,1},{3,2},{4,7},{5,4},{6,5},{7,6},{8,11},{9,8},{10,9... | collective-permute-start | bytes 1179656 | tf_op jit(solution)/shard_map/ppermute | solution.py:26
  71.9 0.9 copy-start.2
  73.6 12.9 %collective-permute-start.3 = (bf16[96,2048]{1,0:T(8,128)(2,1)}, bf16[96,2048]{1,0:T(8,128)(2,1)}, u32[]{:S(2)}, u32[]{:S(2)}) collective-permute-start(bf16[96,2048]{1,0:T(8,128)(2,1)} %slice_bitcast_fusion.1), channel_id=1, source_target_pairs={{0,1},{1,2},{2,3},{3,0},{4,5},{5,6},{6,7},{7,4},{8,9},{9,10},{10,1... | collective-permute-start | bytes 1179656 | tf_op jit(solution)/shard_map/ppermute | solution.py:26
  79.3 45.8 %copy-start = (s32[3]{0:T(128)S(1)}, s32[3]{0:T(128)}, u32[]{:S(2)}) copy-start(s32[3]{0:T(128)} %pad_add_fusion.at_ref) | copy-start | bytes 40
  92.5 7.9 %collective-permute-start.5 = (bf16[8,2,48,2048]{3,2,1,0:T(8,128)(2,1)}, bf16[8,2,48,2048]{3,2,1,0:T(8,128)(2,1)}, u32[]{:S(2)}, u32[]{:S(2)}) collective-permute-start(bf16[8,2,48,2048]{3,2,1,0:T(8,128)(2,1)} %shard_map.56), channel_id=1, source_target_pairs={{0,16},{16,0},{1,17},{17,1},{2,18},{18,2},{3,19},{19,3},{4,20},{20... | collective-permute-start | bytes 9437192 | tf_op jit(solution)/shard_map/ppermute | solution.py:26

commit v5 on v4

--- a/solution.py
+++ b/solution.py
@@ -122,8 +122,8 @@
         slot = source // rows
         move = jnp.where(slot == 1, outer - 1, jnp.where(slot == 2, 1, jnp.where(slot == 3, 2, 0)))
         at_x = (at_ref[0] + move) % outer
-        at_z = source % rows // (high * own)
-        at_high = source % (high * own) // own
+        at_high = source % rows // (deep * own)
+        at_z = source % (deep * own) // own
         goes = at_z * inner + (at_high * outer + at_x) * own + source % own
         pick = jnp.where(to == goes, 1.0, 0.0).astype(jnp.bfloat16)
         for copy in copies:
@@ -223,7 +223,7 @@
     own = queries.shape[0]
     order = (lax.axis_size("z"), lax.axis_size("y_hi"), own)
 
-    line = gather(queries.reshape((-1, 128)), ("z", "y_hi"))
+    line = gather(queries.reshape((-1, 128)), ("y_hi", "z"))
     buffer = prepare(gradients, destinations[None], left_factor, right_factor, bucket, capacity)
     line, buffer = lax.optimization_barrier((line, buffer))
     near = shift(line, "y_lo", 1)

time: 135 us -> 136 us (level)
  transfers between devices with their start and end apart: 8 -> 8, of which waited for: 7 -> 6; matrix products, arithmetic and copies ran while one was open for 5% -> 5% of each run, Pallas kernels for 14% -> 14%
where the time goes in v5:
time: 136 us; the launch traced here: 135 us
  waiting for transfers between devices  57.3 us (42%)
  starting transfers between devices  40.2 us (30%)
  Pallas kernels  27.4 us (20%)
  local copies, waits for them, and re-layouts  9.14 us (7%)
    ppermute x6, waiting for transfers between devices, shift(): lax.ppermute(block, axis, [(i, (i + by) % count) for i in range(count)])  29.2 us
    all_to_all x2, waiting for transfers between devices, exchange(): return lax.all_to_all(block, axis, split_axis=0, concat_axis=0, tiled=True)  28.2 us
    all_to_all x2, starting transfers between devices, exchange(): return lax.all_to_all(block, axis, split_axis=0, concat_axis=0, tiled=True)  22.1 us
    ppermute x6, starting transfers between devices, shift(): lax.ppermute(block, axis, [(i, (i + by) % count) for i in range(count)])  18.1 us
    pallas_call x1, Pallas kernels, prepare(): pl.pallas_call(kernel, grid=(steps + 1,), in_specs=[pl.BlockSpec((1, rows...  12.7 us
    pallas_call x1, Pallas kernels, score(): pl.pallas_call(kernel, grid_spec=pltpu.PrefetchScalarGridSpec(num_scalar_...  8.73 us
    pallas_call x1, Pallas kernels, reorder(): pl.pallas_call(kernel, in_specs=[pl.BlockSpec(memory_space=pltpu.SMEM)] +...  6.02 us
    another operation x3, local copies, waits for them, and re-layouts, body(): pair = jnp.stack([line, near]).reshape((2, -1, width))  2.88 us
  transfers between devices with their start and end apart: 8, of which 6 were waited for; matrix products, arithmetic and copies ran while one was open for 5% of the time, Pallas kernels for 14%

profile of v5, /device:TPU:6, one launch (start us, length us, event | category | flops | bytes accessed | tf_op | source)
XLA Modules:
  0.0 135.0 jit_solution(8032193877740816052)
XLA Ops:
  0.7 0.8 broadcast_in_dim.11
  1.5 16.0 %all-to-all-start = ((bf16[32,48,128]{2,1,0:T(8,128)(2,1)}), bf16[32,48,128]{2,1,0:T(8,128)(2,1)S(1)}, u32[]{:S(2)}, u32[]{:S(2)}) async-start(bf16[32,48,128]{2,1,0:T(8,128)(2,1)} %broadcast_in_dim.11), calls=%async_computation | async-start | bytes 786432 | tf_op jit(solution)/shard_map/all_to_all | solution.py:16
  17.5 1.3 broadcast_in_dim.12.targets_ref
  18.8 12.7 %shard_map.55 = bf16[768,2048]{1,0:T(8,128)(2,1)} custom-call(s32[1,384]{1,0:T(1,128)} %broadcast_in_dim.12.targets_ref, bf16[384,2048]{1,0:T(8,128)(2,1)} %rows_ref.1, f32[32,32]{1,0:T(8,128)} %left_ref.1, f32[64,64]{1,0:T(8,128)} %right_ref.1), custom_call_target="tpu_custom_call" | custom-call | flops 7650410496 | bytes 6291456 | tf_op jit(solution)/shard_map/pallas_call | solution.py:79
  31.5 2.7 %all-to-all-done = bf16[32,48,128]{2,1,0:T(8,128)(2,1)S(1)} async-done(((bf16[32,48,128]{2,1,0:T(8,128)(2,1)}), bf16[32,48,128]{2,1,0:T(8,128)(2,1)S(1)}, u32[]{:S(2)}, u32[]{:S(2)}) %all-to-all-start) | async-done | bytes 393248 | tf_op jit(solution)/shard_map/all_to_all | solution.py:16
  34.2 1.9 %collective-permute-start = (bf16[32,48,128]{2,1,0:T(8,128)(2,1)S(1)}, bf16[32,48,128]{2,1,0:T(8,128)(2,1)}, u32[]{:S(2)}, u32[]{:S(2)}) collective-permute-start(bf16[32,48,128]{2,1,0:T(8,128)(2,1)S(1)} %all-to-all-done), channel_id=1, source_target_pairs={{0,32},{32,0},{1,33},{33,1},{2,34},{34,2},{3,35},{35,3},{4,36},{36... | collective-permute-start | bytes 1179656 | tf_op jit(solution)/shard_map/ppermute | solution.py:26
  36.1 6.1 %all-to-all-start.1 = ((bf16[32,24,2048]{2,1,0:T(8,128)(2,1)}), bf16[32,24,2048]{2,1,0:T(8,128)(2,1)S(1)}, u32[]{:S(2)}, u32[]{:S(2)}) async-start(bf16[32,24,2048]{2,1,0:T(8,128)(2,1)} %bitcast.13), calls=%async_computation.1 | async-start | bytes 6291456 | tf_op jit(solution)/shard_map/all_to_all | solution.py:16
  42.2 0.9 stack.25
  43.1 1.8 %constant_dynamic-update-slice_fusion.1 = bf16[2,96,2048]{2,1,0:T(8,128)(2,1)} fusion(bf16[1,96,2048]{2,1,0:T(8,128)(2,1)} %stack.25), kind=kLoop, calls=%fused_computation.3 | loop fusion | bytes 786432
  44.9 1.2 stack.26
  46.1 0.8 constant_dynamic-update-slice_fusion.pair_ref
  46.9 2.7 %collective-permute-start.2 = (bf16[2,96,2048]{2,1,0:T(8,128)(2,1)}, bf16[2,96,2048]{2,1,0:T(8,128)(2,1)S(1)}, u32[]{:S(2)}, u32[]{:S(2)}) collective-permute-start(bf16[2,96,2048]{2,1,0:T(8,128)(2,1)} %constant_dynamic-update-slice_fusion.pair_ref), channel_id=1, source_target_pairs={{0,3},{1,0},{2,1},{3,2},{4,7},{5,4},{6,5},{7,6},{8,11},{9,8},{10,9... | collective-permute-start | bytes 2359304 | tf_op jit(solution)/shard_map/ppermute | solution.py:26
  49.6 4.3 %collective-permute-start.1 = (bf16[2,96,2048]{2,1,0:T(8,128)(2,1)}, bf16[2,96,2048]{2,1,0:T(8,128)(2,1)S(1)}, u32[]{:S(2)}, u32[]{:S(2)}) collective-permute-start(bf16[2,96,2048]{2,1,0:T(8,128)(2,1)} %constant_dynamic-update-slice_fusion.pair_ref), channel_id=1, source_target_pairs={{0,1},{1,2},{2,3},{3,0},{4,5},{5,6},{6,7},{7,4},{8,9},{9,10},{10,1... | collective-permute-start | bytes 2359304 | tf_op jit(solution)/shard_map/ppermute | solution.py:26
  53.9 16.0 %collective-permute-done.2.after_ref = bf16[2,96,2048]{2,1,0:T(8,128)(2,1)S(1)} collective-permute-done((bf16[2,96,2048]{2,1,0:T(8,128)(2,1)}, bf16[2,96,2048]{2,1,0:T(8,128)(2,1)S(1)}, u32[]{:S(2)}, u32[]{:S(2)}) %collective-permute-start.2) | collective-permute-done | bytes 786464 | tf_op jit(solution)/shard_map/ppermute | solution.py:26
  69.9 1.9 %collective-permute-start.4 = (bf16[96,2048]{1,0:T(8,128)(2,1)S(1)}, bf16[96,2048]{1,0:T(8,128)(2,1)}, u32[]{:S(2)}, u32[]{:S(2)}) collective-permute-start(bf16[96,2048]{1,0:T(8,128)(2,1)S(1)} %slice_bitcast_fusion), channel_id=1, source_target_pairs={{0,3},{1,0},{2,1},{3,2},{4,7},{5,4},{6,5},{7,6},{8,11},{9,8},{10,9... | collective-permute-start | bytes 1179656 | tf_op jit(solution)/shard_map/ppermute | solution.py:26
  71.9 0.9 copy-done.2
  73.5 5.1 %collective-permute-start.3 = (bf16[96,2048]{1,0:T(8,128)(2,1)}, bf16[96,2048]{1,0:T(8,128)(2,1)}, u32[]{:S(2)}, u32[]{:S(2)}) collective-permute-start(bf16[96,2048]{1,0:T(8,128)(2,1)} %slice_bitcast_fusion.1), channel_id=1, source_target_pairs={{0,1},{1,2},{2,3},{3,0},{4,5},{5,6},{6,7},{7,4},{8,9},{9,10},{10,1... | collective-permute-start | bytes 1179656 | tf_op jit(solution)/shard_map/ppermute | solution.py:26
  79.3 4.3 %collective-permute-done.4.far1_ref = bf16[96,2048]{1,0:T(8,128)(2,1)} collective-permute-done((bf16[96,2048]{1,0:T(8,128)(2,1)S(1)}, bf16[96,2048]{1,0:T(8,128)(2,1)}, u32[]{:S(2)}, u32[]{:S(2)}) %collective-permute-start.4) | collective-permute-done | bytes 393248 | tf_op jit(solution)/shard_map/ppermute | solution.py:26
  83.6 3.1 %collective-permute-done.3.far0_ref = bf16[96,2048]{1,0:T(8,128)(2,1)} collective-permute-done((bf16[96,2048]{1,0:T(8,128)(2,1)}, bf16[96,2048]{1,0:T(8,128)(2,1)}, u32[]{:S(2)}, u32[]{:S(2)}) %collective-permute-start.3) | collective-permute-done | bytes 393248 | tf_op jit(solution)/shard_map/ppermute | solution.py:26
  86.7 6.0 %shard_map.56 = bf16[8,2,48,2048]{3,2,1,0:T(8,128)(2,1)} custom-call(s32[3]{0:T(128)} %pad_add_fusion.at_ref, bf16[2,96,2048]{2,1,0:T(8,128)(2,1)} %constant_dynamic-update-slice_fusion.pair_ref, bf16[2,96,2048]{2,1,0:T(8,128)(2,1)} %copy-done.2, bf16[2,96,2048]{2,1,0:T(8,128)(2,1)} %copy-done.1, bf16[96,2048]{1,0:T(8,128)(2,1)} %collective-permute-done.3.far0_ref, ...), custom_call_target="tpu_custom_call" | custom-call | flops 3623878656 | bytes 6291456 | tf_op jit(solution)/shard_map/pallas_call | solution.py:137
  92.7 2.1 %collective-permute-start.5 = (bf16[8,2,48,2048]{3,2,1,0:T(8,128)(2,1)}, bf16[8,2,48,2048]{3,2,1,0:T(8,128)(2,1)}, u32[]{:S(2)}, u32[]{:S(2)}) collective-permute-start(bf16[8,2,48,2048]{3,2,1,0:T(8,128)(2,1)} %shard_map.56), channel_id=1, source_target_pairs={{0,16},{16,0},{1,17},{17,1},{2,18},{18,2},{3,19},{19,3},{4,20},{20... | collective-permute-start | bytes 9437192 | tf_op jit(solution)/shard_map/ppermute | solution.py:26
  94.8 5.8 %collective-permute-done.5 = bf16[8,2,48,2048]{3,2,1,0:T(8,128)(2,1)} collective-permute-done((bf16[8,2,48,2048]{3,2,1,0:T(8,128)(2,1)}, bf16[8,2,48,2048]{3,2,1,0:T(8,128)(2,1)}, u32[]{:S(2)}, u32[]{:S(2)}) %collective-permute-start.5) | collective-permute-done | bytes 3145760 | tf_op jit(solution)/shard_map/ppermute | solution.py:26
  100.6 25.5 %all-to-all-done.1 = bf16[32,24,2048]{2,1,0:T(8,128)(2,1)S(1)} async-done(((bf16[32,24,2048]{2,1,0:T(8,128)(2,1)}), bf16[32,24,2048]{2,1,0:T(8,128)(2,1)S(1)}, u32[]{:S(2)}, u32[]{:S(2)}) %all-to-all-start.1) | async-done | bytes 3145760 | tf_op jit(solution)/shard_map/all_to_all | solution.py:16
  126.1 8.7 %shard_map.57 = bf16[16,2,48,768]{3,2,1,0:T(8,128)(2,1)} custom-call(s32[3]{0:T(128)S(1)} %copy-done, bf16[16,48,2048]{2,1,0:T(8,128)(2,1)} %bitcast.14, bf16[16,48,2048]{2,1,0:T(8,128)(2,1)} %bitcast.6.other_ref, bf16[768,2048]{1,0:T(8,128)(2,1)S(1)} %bitcast.12), custom_call_target="tpu_custom_call" | custom-call | flops 4831838208 | bytes 12582912 | tf_op jit(solution)/shard_map/pallas_call | solution.py:193
  (11 shorter events, 2.2 us)
Async XLA Ops:
  1.5 32.6 %all-to-all-start = ((bf16[32,48,128]{2,1,0:T(8,128)(2,1)}), bf16[32,48,128]{2,1,0:T(8,128)(2,1)S(1)}, u32[]{:S(2)}, u32[]{:S(2)}) async-start(bf16[32,48,128]{2,1,0:T(8,128)(2,1)} %broadcast_in_dim.11), calls=%async_computation | async-start | bytes 786432 | tf_op jit(solution)/shard_map/all_to_all | solution.py:16
  34.2 10.7 %collective-permute-start = (bf16[32,48,128]{2,1,0:T(8,128)(2,1)S(1)}, bf16[32,48,128]{2,1,0:T(8,128)(2,1)}, u32[]{:S(2)}, u32[]{:S(2)}) collective-permute-start(bf16[32,48,128]{2,1,0:T(8,128)(2,1)S(1)} %all-to-all-done), channel_id=1, source_target_pairs={{0,32},{32,0},{1,33},{33,1},{2,34},{34,2},{3,35},{35,3},{4,36},{36... | collective-permute-start | bytes 1179656 | tf_op jit(solution)/shard_map/ppermute | solution.py:26
  36.1 90.0 %all-to-all-start.1 = ((bf16[32,24,2048]{2,1,0:T(8,128)(2,1)}), bf16[32,24,2048]{2,1,0:T(8,128)(2,1)S(1)}, u32[]{:S(2)}, u32[]{:S(2)}) async-start(bf16[32,24,2048]{2,1,0:T(8,128)(2,1)} %bitcast.13), calls=%async_computation.1 | async-start | bytes 6291456 | tf_op jit(solution)/shard_map/all_to_all | solution.py:16
  46.9 23.0 %collective-permute-start.2 = (bf16[2,96,2048]{2,1,0:T(8,128)(2,1)}, bf16[2,96,2048]{2,1,0:T(8,128)(2,1)S(1)}, u32[]{:S(2)}, u32[]{:S(2)}) collective-permute-start(bf16[2,96,2048]{2,1,0:T(8,128)(2,1)} %constant_dynamic-update-slice_fusion.pair_ref), channel_id=1, source_target_pairs={{0,3},{1,0},{2,1},{3,2},{4,7},{5,4},{6,5},{7,6},{8,11},{9,8},{10,9... | collective-permute-start | bytes 2359304 | tf_op jit(solution)/shard_map/ppermute | solution.py:26
  49.6 22.3 %collective-permute-start.1 = (bf16[2,96,2048]{2,1,0:T(8,128)(2,1)}, bf16[2,96,2048]{2,1,0:T(8,128)(2,1)S(1)}, u32[]{:S(2)}, u32[]{:S(2)}) collective-permute-start(bf16[2,96,2048]{2,1,0:T(8,128)(2,1)} %constant_dynamic-update-slice_fusion.pair_ref), channel_id=1, source_target_pairs={{0,1},{1,2},{2,3},{3,0},{4,5},{5,6},{6,7},{7,4},{8,9},{9,10},{10,1... | collective-permute-start | bytes 2359304 | tf_op jit(solution)/shard_map/ppermute | solution.py:26
  69.9 2.0 %copy-start.1 = (bf16[2,96,2048]{2,1,0:T(8,128)(2,1)}, bf16[2,96,2048]{2,1,0:T(8,128)(2,1)S(1)}, u32[]{:S(2)}) copy-start(bf16[2,96,2048]{2,1,0:T(8,128)(2,1)S(1)} %collective-permute-done.2.after_ref) | copy-start | bytes 2359300
  69.9 13.7 %collective-permute-start.4 = (bf16[96,2048]{1,0:T(8,128)(2,1)S(1)}, bf16[96,2048]{1,0:T(8,128)(2,1)}, u32[]{:S(2)}, u32[]{:S(2)}) collective-permute-start(bf16[96,2048]{1,0:T(8,128)(2,1)S(1)} %slice_bitcast_fusion), channel_id=1, source_target_pairs={{0,3},{1,0},{2,1},{3,2},{4,7},{5,4},{6,5},{7,6},{8,11},{9,8},{10,9... | collective-permute-start | bytes 1179656 | tf_op jit(solution)/shard_map/ppermute | solution.py:26
  71.9 0.9 copy-start.2
  73.5 13.1 %collective-permute-start.3 = (bf16[96,2048]{1,0:T(8,128)(2,1)}, bf16[96,2048]{1,0:T(8,128)(2,1)}, u32[]{:S(2)}, u32[]{:S(2)}) collective-permute-start(bf16[96,2048]{1,0:T(8,128)(2,1)} %slice_bitcast_fusion.1), channel_id=1, source_target_pairs={{0,1},{1,2},{2,3},{3,0},{4,5},{5,6},{6,7},{7,4},{8,9},{9,10},{10,1... | collective-permute-start | bytes 1179656 | tf_op jit(solution)/shard_map/ppermute | solution.py:26
  79.3 46.8 %copy-start = (s32[3]{0:T(128)S(1)}, s32[3]{0:T(128)}, u32[]{:S(2)}) copy-start(s32[3]{0:T(128)} %pad_add_fusion.at_ref) | copy-start | bytes 40
  92.7 7.9 %collective-permute-start.5 = (bf16[8,2,48,2048]{3,2,1,0:T(8,128)(2,1)}, bf16[8,2,48,2048]{3,2,1,0:T(8,128)(2,1)}, u32[]{:S(2)}, u32[]{:S(2)}) collective-permute-start(bf16[8,2,48,2048]{3,2,1,0:T(8,128)(2,1)} %shard_map.56), channel_id=1, source_target_pairs={{0,16},{16,0},{1,17},{17,1},{2,18},{18,2},{3,19},{19,3},{4,20},{20... | collective-permute-start | bytes 9437192 | tf_op jit(solution)/shard_map/ppermute | solution.py:26

commit v6 on v4

--- a/solution.py
+++ b/solution.py
@@ -16,9 +16,19 @@
     return lax.all_to_all(block, axis, split_axis=0, concat_axis=0, tiled=True)
 
 
-def gather(block, axis):
-    count = lax.axis_size(axis)
-    return exchange(jnp.broadcast_to(block[None], (count,) + block.shape), axis)
+def copies_of(queries, count):
+    own, width = queries.shape
+    tall = own * width // 128
+
+    def kernel(in_ref, out_ref):
+        whole = in_ref[...].astype(jnp.float32)
+        parts = [whole[q : q + 1, c : c + 128] for q in range(own) for c in range(0, width, 128)]
+        block = jnp.concatenate(parts, axis=0).astype(jnp.bfloat16)
+        out_ref[...] = jnp.broadcast_to(block[None], (count, tall, 128))
+
+    return pl.pallas_call(
+        kernel, out_shape=jax.ShapeDtypeStruct((count, tall, 128), jnp.bfloat16)
+    )(queries)
 
 
 def shift(block, axis, by):
@@ -223,7 +233,7 @@
     own = queries.shape[0]
     order = (lax.axis_size("z"), lax.axis_size("y_hi"), own)
 
-    line = gather(queries.reshape((-1, 128)), ("z", "y_hi"))
+    line = exchange(copies_of(queries, lax.axis_size(("z", "y_hi"))), ("z", "y_hi"))
     buffer = prepare(gradients, destinations[None], left_factor, right_factor, bucket, capacity)
     line, buffer = lax.optimization_barrier((line, buffer))
     near = shift(line, "y_lo", 1)

time: 135 us -> 135 us (level)
  local copies, waits for them, and re-layouts: 9.14 us -> 7.6 us
  Pallas kernels: 27.4 us -> 28.9 us
    broadcast_in_dim x2 -> x0, local copies, waits for them, and re-layouts: 1.54 us -> none  [gather(): return exchange(jnp.broadcast_to(block[None], (count,) + block.shape), axis)]
    pallas_call x0 -> x1, Pallas kernels: none -> 1.5 us  [copies_of(): pl.pallas_call(kernel, out_shape=jax.ShapeDtypeStruct((count, tall, 128),...]
where the time goes in v6:
time: 135 us; the launch traced here: 134 us
  waiting for transfers between devices  56.3 us (42%)
  starting transfers between devices  40.2 us (30%)
  Pallas kernels  28.9 us (21%)
  local copies, waits for them, and re-layouts  7.6 us (6%)
    ppermute x6, waiting for transfers between devices, shift(): lax.ppermute(block, axis, [(i, (i + by) % count) for i in range(count)])  28.9 us
    all_to_all x2, waiting for transfers between devices, exchange(): return lax.all_to_all(block, axis, split_axis=0, concat_axis=0, tiled=True)  27.4 us
    all_to_all x2, starting transfers between devices, exchange(): return lax.all_to_all(block, axis, split_axis=0, concat_axis=0, tiled=True)  22.1 us
    ppermute x6, starting transfers between devices, shift(): lax.ppermute(block, axis, [(i, (i + by) % count) for i in range(count)])  18.1 us
    pallas_call x1, Pallas kernels, prepare(): pl.pallas_call(kernel, grid=(steps + 1,), in_specs=[pl.BlockSpec((1, rows...  12.7 us
    pallas_call x1, Pallas kernels, score(): pl.pallas_call(kernel, grid_spec=pltpu.PrefetchScalarGridSpec(num_scalar_...  8.73 us
    pallas_call x1, Pallas kernels, reorder(): pl.pallas_call(kernel, in_specs=[pl.BlockSpec(memory_space=pltpu.SMEM)] +...  6.02 us
    another operation x3, local copies, waits for them, and re-layouts, body(): pair = jnp.stack([line, near]).reshape((2, -1, width))  2.88 us
  transfers between devices with their start and end apart: 8, of which 7 were waited for; matrix products, arithmetic and copies ran while one was open for 5% of the time, Pallas kernels for 14%

profile of v6, /device:TPU:6, one launch (start us, length us, event | category | flops | bytes accessed | tf_op | source)
XLA Modules:
  0.0 133.9 jit_solution(17354766365713220951)
XLA Ops:
  0.0 1.5 %shard_map.55 = bf16[32,48,128]{2,1,0:T(8,128)(2,1)} custom-call(bf16[3,2048]{1,0:T(4,128)(2,1)} %in_ref.1), custom_call_target="tpu_custom_call" | custom-call | tf_op jit(solution)/shard_map/pallas_call | solution.py:29
  1.5 16.0 %all-to-all-start = ((bf16[32,48,128]{2,1,0:T(8,128)(2,1)}), bf16[32,48,128]{2,1,0:T(8,128)(2,1)S(1)}, u32[]{:S(2)}, u32[]{:S(2)}) async-start(bf16[32,48,128]{2,1,0:T(8,128)(2,1)} %shard_map.55), calls=%async_computation | async-start | bytes 786432 | tf_op jit(solution)/shard_map/all_to_all | solution.py:16
  17.5 1.3 broadcast_in_dim.3.targets_ref
  18.7 12.7 %shard_map.56 = bf16[768,2048]{1,0:T(8,128)(2,1)} custom-call(s32[1,384]{1,0:T(1,128)} %broadcast_in_dim.3.targets_ref, bf16[384,2048]{1,0:T(8,128)(2,1)} %rows_ref.1, f32[32,32]{1,0:T(8,128)} %left_ref.1, f32[64,64]{1,0:T(8,128)} %right_ref.1), custom_call_target="tpu_custom_call" | custom-call | flops 7650410496 | bytes 6291456 | tf_op jit(solution)/shard_map/pallas_call | solution.py:89
  31.4 2.7 %all-to-all-done = bf16[32,48,128]{2,1,0:T(8,128)(2,1)S(1)} async-done(((bf16[32,48,128]{2,1,0:T(8,128)(2,1)}), bf16[32,48,128]{2,1,0:T(8,128)(2,1)S(1)}, u32[]{:S(2)}, u32[]{:S(2)}) %all-to-all-start) | async-done | bytes 393248 | tf_op jit(solution)/shard_map/all_to_all | solution.py:16
  34.1 1.9 %collective-permute-start = (bf16[32,48,128]{2,1,0:T(8,128)(2,1)S(1)}, bf16[32,48,128]{2,1,0:T(8,128)(2,1)}, u32[]{:S(2)}, u32[]{:S(2)}) collective-permute-start(bf16[32,48,128]{2,1,0:T(8,128)(2,1)S(1)} %all-to-all-done), channel_id=1, source_target_pairs={{0,32},{32,0},{1,33},{33,1},{2,34},{34,2},{3,35},{35,3},{4,36},{36... | collective-permute-start | bytes 1179656 | tf_op jit(solution)/shard_map/ppermute | solution.py:36
  36.0 6.1 %all-to-all-start.1 = ((bf16[32,24,2048]{2,1,0:T(8,128)(2,1)}), bf16[32,24,2048]{2,1,0:T(8,128)(2,1)S(1)}, u32[]{:S(2)}, u32[]{:S(2)}) async-start(bf16[32,24,2048]{2,1,0:T(8,128)(2,1)} %bitcast.13), calls=%async_computation.1 | async-start | bytes 6291456 | tf_op jit(solution)/shard_map/all_to_all | solution.py:16
  42.2 0.9 stack.25
  43.1 1.8 %constant_dynamic-update-slice_fusion.1 = bf16[2,96,2048]{2,1,0:T(8,128)(2,1)} fusion(bf16[1,96,2048]{2,1,0:T(8,128)(2,1)} %stack.25), kind=kLoop, calls=%fused_computation.3 | loop fusion | bytes 786432
  45.1 1.2 stack.26
  46.3 0.8 constant_dynamic-update-slice_fusion.pair_ref
  47.1 2.7 %collective-permute-start.2 = (bf16[2,96,2048]{2,1,0:T(8,128)(2,1)}, bf16[2,96,2048]{2,1,0:T(8,128)(2,1)S(1)}, u32[]{:S(2)}, u32[]{:S(2)}) collective-permute-start(bf16[2,96,2048]{2,1,0:T(8,128)(2,1)} %constant_dynamic-update-slice_fusion.pair_ref), channel_id=1, source_target_pairs={{0,3},{1,0},{2,1},{3,2},{4,7},{5,4},{6,5},{7,6},{8,11},{9,8},{10,9... | collective-permute-start | bytes 2359304 | tf_op jit(solution)/shard_map/ppermute | solution.py:36
  49.8 4.3 %collective-permute-start.1 = (bf16[2,96,2048]{2,1,0:T(8,128)(2,1)}, bf16[2,96,2048]{2,1,0:T(8,128)(2,1)S(1)}, u32[]{:S(2)}, u32[]{:S(2)}) collective-permute-start(bf16[2,96,2048]{2,1,0:T(8,128)(2,1)} %constant_dynamic-update-slice_fusion.pair_ref), channel_id=1, source_target_pairs={{0,1},{1,2},{2,3},{3,0},{4,5},{5,6},{6,7},{7,4},{8,9},{9,10},{10,1... | collective-permute-start | bytes 2359304 | tf_op jit(solution)/shard_map/ppermute | solution.py:36
  54.1 15.7 %collective-permute-done.2.after_ref = bf16[2,96,2048]{2,1,0:T(8,128)(2,1)S(1)} collective-permute-done((bf16[2,96,2048]{2,1,0:T(8,128)(2,1)}, bf16[2,96,2048]{2,1,0:T(8,128)(2,1)S(1)}, u32[]{:S(2)}, u32[]{:S(2)}) %collective-permute-start.2) | collective-permute-done | bytes 786464 | tf_op jit(solution)/shard_map/ppermute | solution.py:36
  69.9 1.9 %collective-permute-start.4 = (bf16[96,2048]{1,0:T(8,128)(2,1)S(1)}, bf16[96,2048]{1,0:T(8,128)(2,1)}, u32[]{:S(2)}, u32[]{:S(2)}) collective-permute-start(bf16[96,2048]{1,0:T(8,128)(2,1)S(1)} %slice_bitcast_fusion), channel_id=1, source_target_pairs={{0,3},{1,0},{2,1},{3,2},{4,7},{5,4},{6,5},{7,6},{8,11},{9,8},{10,9... | collective-permute-start | bytes 1179656 | tf_op jit(solution)/shard_map/ppermute | solution.py:36
  71.8 0.9 copy-done.2
  73.5 5.1 %collective-permute-start.3 = (bf16[96,2048]{1,0:T(8,128)(2,1)}, bf16[96,2048]{1,0:T(8,128)(2,1)}, u32[]{:S(2)}, u32[]{:S(2)}) collective-permute-start(bf16[96,2048]{1,0:T(8,128)(2,1)} %slice_bitcast_fusion.1), channel_id=1, source_target_pairs={{0,1},{1,2},{2,3},{3,0},{4,5},{5,6},{6,7},{7,4},{8,9},{9,10},{10,1... | collective-permute-start | bytes 1179656 | tf_op jit(solution)/shard_map/ppermute | solution.py:36
  79.2 4.1 %collective-permute-done.4.far1_ref = bf16[96,2048]{1,0:T(8,128)(2,1)} collective-permute-done((bf16[96,2048]{1,0:T(8,128)(2,1)S(1)}, bf16[96,2048]{1,0:T(8,128)(2,1)}, u32[]{:S(2)}, u32[]{:S(2)}) %collective-permute-start.4) | collective-permute-done | bytes 393248 | tf_op jit(solution)/shard_map/ppermute | solution.py:36
  83.3 3.1 %collective-permute-done.3.far0_ref = bf16[96,2048]{1,0:T(8,128)(2,1)} collective-permute-done((bf16[96,2048]{1,0:T(8,128)(2,1)}, bf16[96,2048]{1,0:T(8,128)(2,1)}, u32[]{:S(2)}, u32[]{:S(2)}) %collective-permute-start.3) | collective-permute-done | bytes 393248 | tf_op jit(solution)/shard_map/ppermute | solution.py:36
  86.4 6.0 %shard_map.57 = bf16[8,2,48,2048]{3,2,1,0:T(8,128)(2,1)} custom-call(s32[3]{0:T(128)} %pad_add_fusion.at_ref, bf16[2,96,2048]{2,1,0:T(8,128)(2,1)} %constant_dynamic-update-slice_fusion.pair_ref, bf16[2,96,2048]{2,1,0:T(8,128)(2,1)} %copy-done.2, bf16[2,96,2048]{2,1,0:T(8,128)(2,1)} %copy-done.1, bf16[96,2048]{1,0:T(8,128)(2,1)} %collective-permute-done.3.far0_ref, ...), custom_call_target="tpu_custom_call" | custom-call | flops 3623878656 | bytes 6291456 | tf_op jit(solution)/shard_map/pallas_call | solution.py:147
  92.4 2.1 %collective-permute-start.5 = (bf16[8,2,48,2048]{3,2,1,0:T(8,128)(2,1)}, bf16[8,2,48,2048]{3,2,1,0:T(8,128)(2,1)}, u32[]{:S(2)}, u32[]{:S(2)}) collective-permute-start(bf16[8,2,48,2048]{3,2,1,0:T(8,128)(2,1)} %shard_map.57), channel_id=1, source_target_pairs={{0,16},{16,0},{1,17},{17,1},{2,18},{18,2},{3,19},{19,3},{4,20},{20... | collective-permute-start | bytes 9437192 | tf_op jit(solution)/shard_map/ppermute | solution.py:36
  94.5 5.8 %collective-permute-done.5 = bf16[8,2,48,2048]{3,2,1,0:T(8,128)(2,1)} collective-permute-done((bf16[8,2,48,2048]{3,2,1,0:T(8,128)(2,1)}, bf16[8,2,48,2048]{3,2,1,0:T(8,128)(2,1)}, u32[]{:S(2)}, u32[]{:S(2)}) %collective-permute-start.5) | collective-permute-done | bytes 3145760 | tf_op jit(solution)/shard_map/ppermute | solution.py:36
  100.3 24.7 %all-to-all-done.1 = bf16[32,24,2048]{2,1,0:T(8,128)(2,1)S(1)} async-done(((bf16[32,24,2048]{2,1,0:T(8,128)(2,1)}), bf16[32,24,2048]{2,1,0:T(8,128)(2,1)S(1)}, u32[]{:S(2)}, u32[]{:S(2)}) %all-to-all-start.1) | async-done | bytes 3145760 | tf_op jit(solution)/shard_map/all_to_all | solution.py:16
  125.0 8.7 %shard_map.58 = bf16[16,2,48,768]{3,2,1,0:T(8,128)(2,1)} custom-call(s32[3]{0:T(128)S(1)} %copy-done, bf16[16,48,2048]{2,1,0:T(8,128)(2,1)} %bitcast.14, bf16[16,48,2048]{2,1,0:T(8,128)(2,1)} %bitcast.6.other_ref, bf16[768,2048]{1,0:T(8,128)(2,1)S(1)} %bitcast.12), custom_call_target="tpu_custom_call" | custom-call | flops 4831838208 | bytes 12582912 | tf_op jit(solution)/shard_map/pallas_call | solution.py:203
  (10 shorter events, 1.7 us)
Async XLA Ops:
  1.5 32.6 %all-to-all-start = ((bf16[32,48,128]{2,1,0:T(8,128)(2,1)}), bf16[32,48,128]{2,1,0:T(8,128)(2,1)S(1)}, u32[]{:S(2)}, u32[]{:S(2)}) async-start(bf16[32,48,128]{2,1,0:T(8,128)(2,1)} %shard_map.55), calls=%async_computation | async-start | bytes 786432 | tf_op jit(solution)/shard_map/all_to_all | solution.py:16
  34.1 11.0 %collective-permute-start = (bf16[32,48,128]{2,1,0:T(8,128)(2,1)S(1)}, bf16[32,48,128]{2,1,0:T(8,128)(2,1)}, u32[]{:S(2)}, u32[]{:S(2)}) collective-permute-start(bf16[32,48,128]{2,1,0:T(8,128)(2,1)S(1)} %all-to-all-done), channel_id=1, source_target_pairs={{0,32},{32,0},{1,33},{33,1},{2,34},{34,2},{3,35},{35,3},{4,36},{36... | collective-permute-start | bytes 1179656 | tf_op jit(solution)/shard_map/ppermute | solution.py:36
  36.0 89.0 %all-to-all-start.1 = ((bf16[32,24,2048]{2,1,0:T(8,128)(2,1)}), bf16[32,24,2048]{2,1,0:T(8,128)(2,1)S(1)}, u32[]{:S(2)}, u32[]{:S(2)}) async-start(bf16[32,24,2048]{2,1,0:T(8,128)(2,1)} %bitcast.13), calls=%async_computation.1 | async-start | bytes 6291456 | tf_op jit(solution)/shard_map/all_to_all | solution.py:16
  47.1 22.8 %collective-permute-start.2 = (bf16[2,96,2048]{2,1,0:T(8,128)(2,1)}, bf16[2,96,2048]{2,1,0:T(8,128)(2,1)S(1)}, u32[]{:S(2)}, u32[]{:S(2)}) collective-permute-start(bf16[2,96,2048]{2,1,0:T(8,128)(2,1)} %constant_dynamic-update-slice_fusion.pair_ref), channel_id=1, source_target_pairs={{0,3},{1,0},{2,1},{3,2},{4,7},{5,4},{6,5},{7,6},{8,11},{9,8},{10,9... | collective-permute-start | bytes 2359304 | tf_op jit(solution)/shard_map/ppermute | solution.py:36
  49.8 22.0 %collective-permute-start.1 = (bf16[2,96,2048]{2,1,0:T(8,128)(2,1)}, bf16[2,96,2048]{2,1,0:T(8,128)(2,1)S(1)}, u32[]{:S(2)}, u32[]{:S(2)}) collective-permute-start(bf16[2,96,2048]{2,1,0:T(8,128)(2,1)} %constant_dynamic-update-slice_fusion.pair_ref), channel_id=1, source_target_pairs={{0,1},{1,2},{2,3},{3,0},{4,5},{5,6},{6,7},{7,4},{8,9},{9,10},{10,1... | collective-permute-start | bytes 2359304 | tf_op jit(solution)/shard_map/ppermute | solution.py:36
  69.8 2.0 %copy-start.1 = (bf16[2,96,2048]{2,1,0:T(8,128)(2,1)}, bf16[2,96,2048]{2,1,0:T(8,128)(2,1)S(1)}, u32[]{:S(2)}) copy-start(bf16[2,96,2048]{2,1,0:T(8,128)(2,1)S(1)} %collective-permute-done.2.after_ref) | copy-start | bytes 2359300
  69.9 13.4 %collective-permute-start.4 = (bf16[96,2048]{1,0:T(8,128)(2,1)S(1)}, bf16[96,2048]{1,0:T(8,128)(2,1)}, u32[]{:S(2)}, u32[]{:S(2)}) collective-permute-start(bf16[96,2048]{1,0:T(8,128)(2,1)S(1)} %slice_bitcast_fusion), channel_id=1, source_target_pairs={{0,3},{1,0},{2,1},{3,2},{4,7},{5,4},{6,5},{7,6},{8,11},{9,8},{10,9... | collective-permute-start | bytes 1179656 | tf_op jit(solution)/shard_map/ppermute | solution.py:36
  71.8 0.9 copy-start.2
  73.5 12.9 %collective-permute-start.3 = (bf16[96,2048]{1,0:T(8,128)(2,1)}, bf16[96,2048]{1,0:T(8,128)(2,1)}, u32[]{:S(2)}, u32[]{:S(2)}) collective-permute-start(bf16[96,2048]{1,0:T(8,128)(2,1)} %slice_bitcast_fusion.1), channel_id=1, source_target_pairs={{0,1},{1,2},{2,3},{3,0},{4,5},{5,6},{6,7},{7,4},{8,9},{9,10},{10,1... | collective-permute-start | bytes 1179656 | tf_op jit(solution)/shard_map/ppermute | solution.py:36
  79.2 45.8 %copy-start = (s32[3]{0:T(128)S(1)}, s32[3]{0:T(128)}, u32[]{:S(2)}) copy-start(s32[3]{0:T(128)} %pad_add_fusion.at_ref) | copy-start | bytes 40
  92.4 7.9 %collective-permute-start.5 = (bf16[8,2,48,2048]{3,2,1,0:T(8,128)(2,1)}, bf16[8,2,48,2048]{3,2,1,0:T(8,128)(2,1)}, u32[]{:S(2)}, u32[]{:S(2)}) collective-permute-start(bf16[8,2,48,2048]{3,2,1,0:T(8,128)(2,1)} %shard_map.57), channel_id=1, source_target_pairs={{0,16},{16,0},{1,17},{17,1},{2,18},{18,2},{3,19},{19,3},{4,20},{20... | collective-permute-start | bytes 9437192 | tf_op jit(solution)/shard_map/ppermute | solution.py:36
